TPU v7x, 256 devices: a whole 4x4x8 slice. The times are simulated.
256 devices in a mesh: seq: 32 (over x, y, core), head: 8 (over z).
Axes of the slice: x: 4, y: 4, z: 8, core: 2. Of those that a mesh axis runs over, the one named last changes fastest.
Arguments:
- hidden: bfloat16 [16384, 2048], P('seq', 'head'), may hold values from -8.5 to 8.5
- w_query: bfloat16 [2048, 2048], P(None, 'head'), may hold values from -0.125 to 0.125
- w_key: bfloat16 [2048, 2048], P(None, 'head'), may hold values from -0.125 to 0.125
- w_value: bfloat16 [2048, 4096], P(None, 'head'), may hold values from -0.125 to 0.125
- conv_query: bfloat16 [4, 2048], P(None, 'head'), may hold values from -3 to 3
- conv_key: bfloat16 [4, 2048], P(None, 'head'), may hold values from -3 to 3
- conv_value: bfloat16 [4, 4096], P(None, 'head'), may hold values from -3 to 3
- gate_log: float32 [32, 16384], P('head', 'seq'), may hold values from -2.5 to 0, as said below
- strength: float32 [32, 16384], P('head', 'seq'), may hold values from 0 to 1, as said below
- initial_state: float32 [32, 128, 128], P('head'), may hold values from -24 to 24
Outputs:
- core_out: bfloat16 [16384, 4096], P('seq', 'head')
- block_states: float32 [32, 32, 128, 128], P('seq', 'head')
Inputs may be any that keep to these rules, and one draw needn't show every extreme that they name: `gate_log`: negative or zero. `strength`: Positive.
All inputs are finite; a program needn't handle non-finite values.
Results may differ from a plain program's by a relative error of at most 0.015.
Values may be sent and summed in bfloat16 or wider, within the bound.
A program may use at most 128 MiB of HBM per device.

v0:
```python
import jax
import jax.numpy as jnp
from jax import lax
from jax.sharding import PartitionSpec as P

DK = 128
DV = 128
SUB = 128


def passed_along(block, axis, distance):
    devices = range(lax.axis_size(axis))
    route = [(i - distance, i) for i in devices if i - distance in devices]
    return lax.ppermute(block, axis, route)


def conv_silu(inputs, prior_rows, kernel):
    length = kernel.shape[0]
    padded = jnp.concatenate([prior_rows, inputs], axis=0)
    running = jnp.zeros(inputs.shape, jnp.float32)
    for tap_index in range(length):
        running = running + kernel[tap_index].astype(jnp.float32) * padded[
            tap_index : tap_index + inputs.shape[0]
        ].astype(jnp.float32)
    return jax.nn.silu(running).astype(jnp.bfloat16)


def unit_heads(inputs, head_count, factor):
    shaped = inputs.reshape(inputs.shape[0], head_count, -1).astype(jnp.float32)
    squares = jnp.sum(shaped * shaped, axis=-1, keepdims=True)
    return (shaped / jnp.sqrt(squares + 1e-06) * factor).astype(jnp.bfloat16)


def matmul_heads(left, right):
    return jnp.einsum("hij,hjk->hik", left, right, precision=lax.Precision.HIGHEST)


def body(
    hidden,
    w_query,
    w_key,
    w_value,
    conv_query,
    conv_key,
    conv_value,
    gate_log,
    strength,
    initial_state,
):
    highest = lax.Precision.HIGHEST
    tokens_here = hidden.shape[0]
    heads = gate_log.shape[0]
    key_heads = w_query.shape[1] // DK
    q_columns = w_query.shape[1]
    piece = lax.all_gather(hidden, "head", axis=1, tiled=True)
    q_sum, k_sum, v_sum = tuple(
        (
            jnp.dot(piece, weight, preferred_element_type=jnp.float32)
            for weight in (w_query, w_key, w_value)
        )
    )
    q_proj = q_sum.astype(jnp.bfloat16)
    k_proj = k_sum.astype(jnp.bfloat16)
    v_proj = v_sum.astype(jnp.bfloat16)
    kept = conv_query.shape[0] - 1
    last_rows = jnp.concatenate(
        [q_proj[tokens_here - kept :], k_proj[tokens_here - kept :], v_proj[tokens_here - kept :]],
        axis=1,
    )
    prior_rows = passed_along(last_rows, "seq", 1)
    q_conv = conv_silu(q_proj, prior_rows[:, :q_columns], conv_query)
    k_conv = conv_silu(k_proj, prior_rows[:, q_columns : 2 * q_columns], conv_key)
    v_conv = conv_silu(v_proj, prior_rows[:, 2 * q_columns :], conv_value)
    q_norm = unit_heads(q_conv, key_heads, DK ** (-0.5))
    k_norm = unit_heads(k_conv, key_heads, 1.0)
    per_key = heads // key_heads
    blocks_here = tokens_here // SUB

    def arrange(inputs):
        return jnp.transpose(
            inputs.reshape(blocks_here, SUB, inputs.shape[1], inputs.shape[2]), (0, 2, 1, 3)
        )

    queries = arrange(jnp.repeat(q_norm, per_key, axis=1))
    keys = arrange(jnp.repeat(k_norm, per_key, axis=1))
    values = arrange(v_conv.reshape(tokens_here, heads, DV))
    log_gates = jnp.transpose(gate_log.reshape(heads, blocks_here, SUB), (1, 0, 2))
    strengths = jnp.transpose(strength.reshape(heads, blocks_here, SUB), (1, 0, 2))
    log_decay = jnp.cumsum(log_gates, axis=-1)
    retain = jnp.exp(log_decay)
    row_ids = lax.broadcasted_iota(jnp.int32, (SUB, SUB), 0)
    col_ids = lax.broadcasted_iota(jnp.int32, (SUB, SUB), 1)
    on_or_below = row_ids >= col_ids
    below = row_ids > col_ids
    spread = log_decay[..., :, None] - log_decay[..., None, :]
    decay = jnp.where(on_or_below, jnp.exp(jnp.where(on_or_below, spread, 0.0)), 0.0)
    key_gram = jnp.einsum("nhta,nhsa->nhts", keys, keys, preferred_element_type=jnp.float32)
    query_key = jnp.einsum("nhta,nhsa->nhts", queries, keys, preferred_element_type=jnp.float32)
    system = (
        jnp.eye(SUB, dtype=jnp.float32)
        + jnp.where(below, decay * key_gram, 0.0) * strengths[..., None]
    )
    keys_f = keys.astype(jnp.float32)
    right_side = jnp.concatenate(
        [
            strengths[..., None] * values.astype(jnp.float32),
            (strengths * retain)[..., None] * keys_f,
        ],
        axis=-1,
    )
    solved = jax.scipy.linalg.solve_triangular(system, right_side, lower=True, unit_diagonal=True)
    local_updates = solved[..., :DV]
    corrections = solved[..., DV:]
    query_mix = decay * query_key
    local_out = jnp.einsum("nhts,nhsv->nhtv", query_mix, local_updates, precision=highest)
    query_eff = retain[..., None] * queries.astype(jnp.float32) - jnp.einsum(
        "nhts,nhsa->nhta", query_mix, corrections, precision=highest
    )
    to_end = jnp.exp(log_decay[..., -1:] - log_decay)
    weighted = keys_f * to_end[..., None]
    transition = retain[..., -1, None, None] * jnp.eye(DK, dtype=jnp.float32) - jnp.einsum(
        "nhta,nhtb->nhab", weighted, corrections, precision=highest
    )
    offset = jnp.einsum("nhta,nhtv->nhav", weighted, local_updates, precision=highest)
    zero_state = jnp.zeros((heads, DK, DV), jnp.float32)
    identity = jnp.broadcast_to(jnp.eye(DK, dtype=jnp.float32), (heads, DK, DK))

    def carry_step(carry, block):
        state, product = carry
        out_block, eff_block, trans_block, offset_block = block
        result = out_block + matmul_heads(eff_block, state)
        moved = matmul_heads(eff_block, product)
        return (
            (matmul_heads(trans_block, state) + offset_block, matmul_heads(trans_block, product)),
            (result, moved),
        )

    (shard_offset, shard_trans), (partial_out, reach_map) = lax.scan(
        carry_step, (zero_state, identity), (local_out, query_eff, transition, offset)
    )
    at_start = lax.axis_index("seq") == 0

    def relay_step(step_index, current):
        outgoing = matmul_heads(shard_trans, current) + shard_offset
        received = passed_along(outgoing, "seq", 1)
        return jnp.where(at_start, initial_state, received)

    incoming = lax.fori_loop(0, lax.axis_size("seq") - 1, relay_step, initial_state)
    core_rows = partial_out + jnp.einsum("nhta,hav->nhtv", reach_map, incoming, precision=highest)
    closing = matmul_heads(shard_trans, incoming) + shard_offset
    core_out = (
        jnp.transpose(core_rows, (0, 2, 1, 3)).reshape(tokens_here, heads * DV).astype(jnp.bfloat16)
    )
    return (core_out, closing[None])


def solution(mesh):
    return jax.shard_map(
        body,
        mesh=mesh,
        in_specs=(
            P("seq", "head"),
            P(None, "head"),
            P(None, "head"),
            P(None, "head"),
            P(None, "head"),
            P(None, "head"),
            P(None, "head"),
            P("head", "seq"),
            P("head", "seq"),
            P("head", None, None),
        ),
        out_specs=(P("seq", "head"), P("seq", "head", None, None)),
        check_vma=False,
    )
```

profile of v0, /device:TPU:7, one launch (start us, length us, event | category | flops | bytes accessed | tf_op | source)
XLA Modules:
  0.0 617.5 jit_solution(10599625248382074952)
XLA Ops:
  7.9 2.3 reduce_window_sum.11
  16.8 39.5 %all-gather.2.cloned.1.call-done = bf16[512,2048]{1,0:T(8,128)(2,1)} async-done(((bf16[512,256]{1,0:T(8,128)(2,1)}), bf16[512,2048]{1,0:T(8,128)(2,1)}) %all-gather.2.cloned.1.call-update) | async-done | bytes 2097168 | tf_op jit(solution)/shard_map/all_gather | solution.py:55
  56.2 3.0 convolution_convert_fusion
  61.4 7.3 %collective-permute-start.1 = (bf16[3,1024]{1,0:T(4,128)(2,1)S(1)}, bf16[3,1024]{1,0:T(4,128)(2,1)S(1)}, u32[]{:S(2)}, u32[]{:S(2)}) collective-permute-start(bf16[3,1024]{1,0:T(4,128)(2,1)S(1)} %pad_maximum_fusion.3), channel_id=1, source_target_pairs={{0,8},{8,16},{16,24},{24,32},{32,40},{40,48},{48,56},{56,64},{64,7... | collective-permute-start | bytes 18440 | tf_op jit(solution)/shard_map/ppermute | solution.py:14
  70.1 2.2 fusion.64
  80.8 158.6 %custom-call.4 = f32[4,4,1,128,128]{3,4,2,1,0:T(8,128)} custom-call(f32[4,4,1,128,128]{4,3,2,1,0:T(8,128)} %fusion.32), custom_call_target="InvertDiagBlocksLowerTriangular" | custom-call | tf_op jit(solution)/shard_map/jit(_solve_triangular)/vmap(vmap())/triangular_solve | solution.py:111
  241.5 3.5 fusion.53
  245.0 2.6 reshape.74
  251.5 2.3 convolution_subtract_fusion
  255.9 3.2 fusion.35
  259.1 3.2 convolution_subtract_fusion.1
  262.4 29.1 %while.28 = (s32[]{:T(128)}, f32[4,128,128]{2,1,0:T(8,128)S(1)}, f32[4,128,128]{2,1,0:T(8,128)S(1)}, f32[4,4,128,128]{2,3,0,1:T(8,128)}, f32[4,4,128,128]{3,2,0,...) while((s32[]{:T(128)}, f32[4,128,128]{2,1,0:T(8,128)S(1)}, ...), condition=%wide.region_4.5_spmd.clone, body=%wide.region_3.4_spmd.clone.sunk | while | flops 402915328 | bytes 5771384 | solution.py:138
  291.5 314.3 %while.27 = (s32[]{:T(128)}, f32[4,128,128]{2,1,0:T(8,128)S(1)}, pred[]{:T(512)}, f32[4,128,128]{2,1,0:T(8,128)S(1)}, f32[4,128,128]{2,1,0:T(8,128)S(1)}, /*index=5*/f32[4,128,128]{2,1,0:T(8,128)}, s32[]{:T(128)}) while((s32[]{:T(128)}, f32[4,128,128]{2,1,0:T(8,128)S(1)}, pred[]{:T(512)}, f32[4,128,128]{2,1,0:T(8,128)S(1)}, ...), condition=%wide.region_6.7_spmd, body=%wide.region_5.6_spmd.sunk | while | flops 100794368 | bytes 2883702 | solution.py:148
  291.9 4.2 collective-permute-start
  296.1 3.3 collective-permute-done
  299.8 4.4 collective-permute-start
  304.2 4.1 collective-permute-done
  308.8 3.5 collective-permute-start
  312.4 6.2 %collective-permute-done = f32[4,128,128]{2,1,0:T(8,128)S(1)} collective-permute-done((f32[4,128,128]{2,1,0:T(8,128)S(1)}, f32[4,128,128]{2,1,0:T(8,128)S(1)}, u32[]{:S(2)}, u32[]{:S(2)}) %collective-permute-start) | collective-permute-done | bytes 262176 | tf_op jit(solution)/shard_map/while/body/eval_jaxpr/ppermute | solution.py:14
  321.0 7.9 %collective-permute-done = f32[4,128,128]{2,1,0:T(8,128)S(1)} collective-permute-done((f32[4,128,128]{2,1,0:T(8,128)S(1)}, f32[4,128,128]{2,1,0:T(8,128)S(1)}, u32[]{:S(2)}, u32[]{:S(2)}) %collective-permute-start) | collective-permute-done | bytes 262176 | tf_op jit(solution)/shard_map/while/body/eval_jaxpr/ppermute | solution.py:14
  331.3 7.9 %collective-permute-done = f32[4,128,128]{2,1,0:T(8,128)S(1)} collective-permute-done((f32[4,128,128]{2,1,0:T(8,128)S(1)}, f32[4,128,128]{2,1,0:T(8,128)S(1)}, u32[]{:S(2)}, u32[]{:S(2)}) %collective-permute-start) | collective-permute-done | bytes 262176 | tf_op jit(solution)/shard_map/while/body/eval_jaxpr/ppermute | solution.py:14
  341.5 7.9 %collective-permute-done = f32[4,128,128]{2,1,0:T(8,128)S(1)} collective-permute-done((f32[4,128,128]{2,1,0:T(8,128)S(1)}, f32[4,128,128]{2,1,0:T(8,128)S(1)}, u32[]{:S(2)}, u32[]{:S(2)}) %collective-permute-start) | collective-permute-done | bytes 262176 | tf_op jit(solution)/shard_map/while/body/eval_jaxpr/ppermute | solution.py:14
  351.8 7.9 %collective-permute-done = f32[4,128,128]{2,1,0:T(8,128)S(1)} collective-permute-done((f32[4,128,128]{2,1,0:T(8,128)S(1)}, f32[4,128,128]{2,1,0:T(8,128)S(1)}, u32[]{:S(2)}, u32[]{:S(2)}) %collective-permute-start) | collective-permute-done | bytes 262176 | tf_op jit(solution)/shard_map/while/body/eval_jaxpr/ppermute | solution.py:14
  362.0 7.9 %collective-permute-done = f32[4,128,128]{2,1,0:T(8,128)S(1)} collective-permute-done((f32[4,128,128]{2,1,0:T(8,128)S(1)}, f32[4,128,128]{2,1,0:T(8,128)S(1)}, u32[]{:S(2)}, u32[]{:S(2)}) %collective-permute-start) | collective-permute-done | bytes 262176 | tf_op jit(solution)/shard_map/while/body/eval_jaxpr/ppermute | solution.py:14
  372.3 7.9 %collective-permute-done = f32[4,128,128]{2,1,0:T(8,128)S(1)} collective-permute-done((f32[4,128,128]{2,1,0:T(8,128)S(1)}, f32[4,128,128]{2,1,0:T(8,128)S(1)}, u32[]{:S(2)}, u32[]{:S(2)}) %collective-permute-start) | collective-permute-done | bytes 262176 | tf_op jit(solution)/shard_map/while/body/eval_jaxpr/ppermute | solution.py:14
  382.5 7.9 %collective-permute-done = f32[4,128,128]{2,1,0:T(8,128)S(1)} collective-permute-done((f32[4,128,128]{2,1,0:T(8,128)S(1)}, f32[4,128,128]{2,1,0:T(8,128)S(1)}, u32[]{:S(2)}, u32[]{:S(2)}) %collective-permute-start) | collective-permute-done | bytes 262176 | tf_op jit(solution)/shard_map/while/body/eval_jaxpr/ppermute | solution.py:14
  392.8 7.9 %collective-permute-done = f32[4,128,128]{2,1,0:T(8,128)S(1)} collective-permute-done((f32[4,128,128]{2,1,0:T(8,128)S(1)}, f32[4,128,128]{2,1,0:T(8,128)S(1)}, u32[]{:S(2)}, u32[]{:S(2)}) %collective-permute-start) | collective-permute-done | bytes 262176 | tf_op jit(solution)/shard_map/while/body/eval_jaxpr/ppermute | solution.py:14
  403.0 7.9 %collective-permute-done = f32[4,128,128]{2,1,0:T(8,128)S(1)} collective-permute-done((f32[4,128,128]{2,1,0:T(8,128)S(1)}, f32[4,128,128]{2,1,0:T(8,128)S(1)}, u32[]{:S(2)}, u32[]{:S(2)}) %collective-permute-start) | collective-permute-done | bytes 262176 | tf_op jit(solution)/shard_map/while/body/eval_jaxpr/ppermute | solution.py:14
  413.3 7.9 %collective-permute-done = f32[4,128,128]{2,1,0:T(8,128)S(1)} collective-permute-done((f32[4,128,128]{2,1,0:T(8,128)S(1)}, f32[4,128,128]{2,1,0:T(8,128)S(1)}, u32[]{:S(2)}, u32[]{:S(2)}) %collective-permute-start) | collective-permute-done | bytes 262176 | tf_op jit(solution)/shard_map/while/body/eval_jaxpr/ppermute | solution.py:14
  423.5 7.9 %collective-permute-done = f32[4,128,128]{2,1,0:T(8,128)S(1)} collective-permute-done((f32[4,128,128]{2,1,0:T(8,128)S(1)}, f32[4,128,128]{2,1,0:T(8,128)S(1)}, u32[]{:S(2)}, u32[]{:S(2)}) %collective-permute-start) | collective-permute-done | bytes 262176 | tf_op jit(solution)/shard_map/while/body/eval_jaxpr/ppermute | solution.py:14
  433.8 7.9 %collective-permute-done = f32[4,128,128]{2,1,0:T(8,128)S(1)} collective-permute-done((f32[4,128,128]{2,1,0:T(8,128)S(1)}, f32[4,128,128]{2,1,0:T(8,128)S(1)}, u32[]{:S(2)}, u32[]{:S(2)}) %collective-permute-start) | collective-permute-done | bytes 262176 | tf_op jit(solution)/shard_map/while/body/eval_jaxpr/ppermute | solution.py:14
  444.0 7.9 %collective-permute-done = f32[4,128,128]{2,1,0:T(8,128)S(1)} collective-permute-done((f32[4,128,128]{2,1,0:T(8,128)S(1)}, f32[4,128,128]{2,1,0:T(8,128)S(1)}, u32[]{:S(2)}, u32[]{:S(2)}) %collective-permute-start) | collective-permute-done | bytes 262176 | tf_op jit(solution)/shard_map/while/body/eval_jaxpr/ppermute | solution.py:14
  454.3 7.9 %collective-permute-done = f32[4,128,128]{2,1,0:T(8,128)S(1)} collective-permute-done((f32[4,128,128]{2,1,0:T(8,128)S(1)}, f32[4,128,128]{2,1,0:T(8,128)S(1)}, u32[]{:S(2)}, u32[]{:S(2)}) %collective-permute-start) | collective-permute-done | bytes 262176 | tf_op jit(solution)/shard_map/while/body/eval_jaxpr/ppermute | solution.py:14
  464.6 7.9 %collective-permute-done = f32[4,128,128]{2,1,0:T(8,128)S(1)} collective-permute-done((f32[4,128,128]{2,1,0:T(8,128)S(1)}, f32[4,128,128]{2,1,0:T(8,128)S(1)}, u32[]{:S(2)}, u32[]{:S(2)}) %collective-permute-start) | collective-permute-done | bytes 262176 | tf_op jit(solution)/shard_map/while/body/eval_jaxpr/ppermute | solution.py:14
  474.8 7.9 %collective-permute-done = f32[4,128,128]{2,1,0:T(8,128)S(1)} collective-permute-done((f32[4,128,128]{2,1,0:T(8,128)S(1)}, f32[4,128,128]{2,1,0:T(8,128)S(1)}, u32[]{:S(2)}, u32[]{:S(2)}) %collective-permute-start) | collective-permute-done | bytes 262176 | tf_op jit(solution)/shard_map/while/body/eval_jaxpr/ppermute | solution.py:14
  485.1 7.9 %collective-permute-done = f32[4,128,128]{2,1,0:T(8,128)S(1)} collective-permute-done((f32[4,128,128]{2,1,0:T(8,128)S(1)}, f32[4,128,128]{2,1,0:T(8,128)S(1)}, u32[]{:S(2)}, u32[]{:S(2)}) %collective-permute-start) | collective-permute-done | bytes 262176 | tf_op jit(solution)/shard_map/while/body/eval_jaxpr/ppermute | solution.py:14
  495.3 7.9 %collective-permute-done = f32[4,128,128]{2,1,0:T(8,128)S(1)} collective-permute-done((f32[4,128,128]{2,1,0:T(8,128)S(1)}, f32[4,128,128]{2,1,0:T(8,128)S(1)}, u32[]{:S(2)}, u32[]{:S(2)}) %collective-permute-start) | collective-permute-done | bytes 262176 | tf_op jit(solution)/shard_map/while/body/eval_jaxpr/ppermute | solution.py:14
  505.6 7.9 %collective-permute-done = f32[4,128,128]{2,1,0:T(8,128)S(1)} collective-permute-done((f32[4,128,128]{2,1,0:T(8,128)S(1)}, f32[4,128,128]{2,1,0:T(8,128)S(1)}, u32[]{:S(2)}, u32[]{:S(2)}) %collective-permute-start) | collective-permute-done | bytes 262176 | tf_op jit(solution)/shard_map/while/body/eval_jaxpr/ppermute | solution.py:14
  515.8 7.9 %collective-permute-done = f32[4,128,128]{2,1,0:T(8,128)S(1)} collective-permute-done((f32[4,128,128]{2,1,0:T(8,128)S(1)}, f32[4,128,128]{2,1,0:T(8,128)S(1)}, u32[]{:S(2)}, u32[]{:S(2)}) %collective-permute-start) | collective-permute-done | bytes 262176 | tf_op jit(solution)/shard_map/while/body/eval_jaxpr/ppermute | solution.py:14
  526.1 7.9 %collective-permute-done = f32[4,128,128]{2,1,0:T(8,128)S(1)} collective-permute-done((f32[4,128,128]{2,1,0:T(8,128)S(1)}, f32[4,128,128]{2,1,0:T(8,128)S(1)}, u32[]{:S(2)}, u32[]{:S(2)}) %collective-permute-start) | collective-permute-done | bytes 262176 | tf_op jit(solution)/shard_map/while/body/eval_jaxpr/ppermute | solution.py:14
  536.3 7.9 %collective-permute-done = f32[4,128,128]{2,1,0:T(8,128)S(1)} collective-permute-done((f32[4,128,128]{2,1,0:T(8,128)S(1)}, f32[4,128,128]{2,1,0:T(8,128)S(1)}, u32[]{:S(2)}, u32[]{:S(2)}) %collective-permute-start) | collective-permute-done | bytes 262176 | tf_op jit(solution)/shard_map/while/body/eval_jaxpr/ppermute | solution.py:14
  546.6 7.9 %collective-permute-done = f32[4,128,128]{2,1,0:T(8,128)S(1)} collective-permute-done((f32[4,128,128]{2,1,0:T(8,128)S(1)}, f32[4,128,128]{2,1,0:T(8,128)S(1)}, u32[]{:S(2)}, u32[]{:S(2)}) %collective-permute-start) | collective-permute-done | bytes 262176 | tf_op jit(solution)/shard_map/while/body/eval_jaxpr/ppermute | solution.py:14
  556.8 7.9 %collective-permute-done = f32[4,128,128]{2,1,0:T(8,128)S(1)} collective-permute-done((f32[4,128,128]{2,1,0:T(8,128)S(1)}, f32[4,128,128]{2,1,0:T(8,128)S(1)}, u32[]{:S(2)}, u32[]{:S(2)}) %collective-permute-start) | collective-permute-done | bytes 262176 | tf_op jit(solution)/shard_map/while/body/eval_jaxpr/ppermute | solution.py:14
  567.1 7.9 %collective-permute-done = f32[4,128,128]{2,1,0:T(8,128)S(1)} collective-permute-done((f32[4,128,128]{2,1,0:T(8,128)S(1)}, f32[4,128,128]{2,1,0:T(8,128)S(1)}, u32[]{:S(2)}, u32[]{:S(2)}) %collective-permute-start) | collective-permute-done | bytes 262176 | tf_op jit(solution)/shard_map/while/body/eval_jaxpr/ppermute | solution.py:14
  577.3 7.9 %collective-permute-done = f32[4,128,128]{2,1,0:T(8,128)S(1)} collective-permute-done((f32[4,128,128]{2,1,0:T(8,128)S(1)}, f32[4,128,128]{2,1,0:T(8,128)S(1)}, u32[]{:S(2)}, u32[]{:S(2)}) %collective-permute-start) | collective-permute-done | bytes 262176 | tf_op jit(solution)/shard_map/while/body/eval_jaxpr/ppermute | solution.py:14
  587.6 7.9 %collective-permute-done = f32[4,128,128]{2,1,0:T(8,128)S(1)} collective-permute-done((f32[4,128,128]{2,1,0:T(8,128)S(1)}, f32[4,128,128]{2,1,0:T(8,128)S(1)}, u32[]{:S(2)}, u32[]{:S(2)}) %collective-permute-start) | collective-permute-done | bytes 262176 | tf_op jit(solution)/shard_map/while/body/eval_jaxpr/ppermute | solution.py:14
  597.8 7.9 %collective-permute-done = f32[4,128,128]{2,1,0:T(8,128)S(1)} collective-permute-done((f32[4,128,128]{2,1,0:T(8,128)S(1)}, f32[4,128,128]{2,1,0:T(8,128)S(1)}, u32[]{:S(2)}, u32[]{:S(2)}) %collective-permute-start) | collective-permute-done | bytes 262176 | tf_op jit(solution)/shard_map/while/body/eval_jaxpr/ppermute | solution.py:14
  606.9 2.6 fusion.36
  (196 shorter events, 125.1 us)
Async XLA Ops:
  7.2 49.0 %copy-start = (bf16[2048,512]{1,0:T(8,128)(2,1)S(1)}, bf16[2048,512]{1,0:T(8,128)(2,1)}, u32[]{:S(2)}) copy-start(bf16[2048,512]{1,0:T(8,128)(2,1)} %param.17) | copy-start | bytes 6291460
  7.2 49.0 %all-gather.2.cloned.1.call-start = ((), (), s32[]{:S(2)}) async-start(), calls=%async_computation | async-start | bytes 2359296 | tf_op jit(solution)/shard_map/all_gather | solution.py:55
  56.2 3.0 copy-start.11
  56.2 3.0 copy-start.12
  59.2 2.1 copy-start.6
  59.2 1.4 copy-start.13
  61.4 8.1 %collective-permute-start.1 = (bf16[3,1024]{1,0:T(4,128)(2,1)S(1)}, bf16[3,1024]{1,0:T(4,128)(2,1)S(1)}, u32[]{:S(2)}, u32[]{:S(2)}) collective-permute-start(bf16[3,1024]{1,0:T(4,128)(2,1)S(1)} %pad_maximum_fusion.3), channel_id=1, source_target_pairs={{0,8},{8,16},{16,24},{24,32},{32,40},{40,48},{48,56},{56,64},{64,7... | collective-permute-start | bytes 18440 | tf_op jit(solution)/shard_map/ppermute | solution.py:14
  69.5 0.6 copy-start.10
  76.0 1.5 copy-start.5
  77.6 1.6 copy-start.7
  77.6 1.6 copy-start.8
  77.6 1.6 copy-start.9
  247.6 1.7 copy-start.3
  247.6 1.9 copy-start.4
  249.4 2.0 copy-start.2
  262.3 29.1 %copy-start.1 = (f32[4,128,128]{2,1,0:T(8,128)S(1)}, f32[4,128,128]{2,1,0:T(8,128)}, u32[]{:S(2)}) copy-start(f32[4,128,128]{2,1,0:T(8,128)} %param.23) | copy-start | bytes 786436
  291.9 7.5 %collective-permute-start = (f32[4,128,128]{2,1,0:T(8,128)S(1)}, f32[4,128,128]{2,1,0:T(8,128)S(1)}, u32[]{:S(2)}, u32[]{:S(2)}) collective-permute-start(f32[4,128,128]{2,1,0:T(8,128)S(1)} %convolution_add_fusion.6), channel_id=1, source_target_pairs={{0,8},{8,16},{16,24},{24,32},{32,40},{40,48},{48,56},{56,64},{64,7... | collective-permute-start | bytes 786440 | tf_op jit(solution)/shard_map/while/body/eval_jaxpr/ppermute | solution.py:14
  299.8 8.5 %collective-permute-start = (f32[4,128,128]{2,1,0:T(8,128)S(1)}, f32[4,128,128]{2,1,0:T(8,128)S(1)}, u32[]{:S(2)}, u32[]{:S(2)}) collective-permute-start(f32[4,128,128]{2,1,0:T(8,128)S(1)} %convolution_add_fusion.6), channel_id=1, source_target_pairs={{0,8},{8,16},{16,24},{24,32},{32,40},{40,48},{48,56},{56,64},{64,7... | collective-permute-start | bytes 786440 | tf_op jit(solution)/shard_map/while/body/eval_jaxpr/ppermute | solution.py:14
  308.8 9.8 %collective-permute-start = (f32[4,128,128]{2,1,0:T(8,128)S(1)}, f32[4,128,128]{2,1,0:T(8,128)S(1)}, u32[]{:S(2)}, u32[]{:S(2)}) collective-permute-start(f32[4,128,128]{2,1,0:T(8,128)S(1)} %convolution_add_fusion.6), channel_id=1, source_target_pairs={{0,8},{8,16},{16,24},{24,32},{32,40},{40,48},{48,56},{56,64},{64,7... | collective-permute-start | bytes 786440 | tf_op jit(solution)/shard_map/while/body/eval_jaxpr/ppermute | solution.py:14
  319.1 9.8 %collective-permute-start = (f32[4,128,128]{2,1,0:T(8,128)S(1)}, f32[4,128,128]{2,1,0:T(8,128)S(1)}, u32[]{:S(2)}, u32[]{:S(2)}) collective-permute-start(f32[4,128,128]{2,1,0:T(8,128)S(1)} %convolution_add_fusion.6), channel_id=1, source_target_pairs={{0,8},{8,16},{16,24},{24,32},{32,40},{40,48},{48,56},{56,64},{64,7... | collective-permute-start | bytes 786440 | tf_op jit(solution)/shard_map/while/body/eval_jaxpr/ppermute | solution.py:14
  329.3 9.8 %collective-permute-start = (f32[4,128,128]{2,1,0:T(8,128)S(1)}, f32[4,128,128]{2,1,0:T(8,128)S(1)}, u32[]{:S(2)}, u32[]{:S(2)}) collective-permute-start(f32[4,128,128]{2,1,0:T(8,128)S(1)} %convolution_add_fusion.6), channel_id=1, source_target_pairs={{0,8},{8,16},{16,24},{24,32},{32,40},{40,48},{48,56},{56,64},{64,7... | collective-permute-start | bytes 786440 | tf_op jit(solution)/shard_map/while/body/eval_jaxpr/ppermute | solution.py:14
  339.6 9.8 %collective-permute-start = (f32[4,128,128]{2,1,0:T(8,128)S(1)}, f32[4,128,128]{2,1,0:T(8,128)S(1)}, u32[]{:S(2)}, u32[]{:S(2)}) collective-permute-start(f32[4,128,128]{2,1,0:T(8,128)S(1)} %convolution_add_fusion.6), channel_id=1, source_target_pairs={{0,8},{8,16},{16,24},{24,32},{32,40},{40,48},{48,56},{56,64},{64,7... | collective-permute-start | bytes 786440 | tf_op jit(solution)/shard_map/while/body/eval_jaxpr/ppermute | solution.py:14
  349.8 9.8 %collective-permute-start = (f32[4,128,128]{2,1,0:T(8,128)S(1)}, f32[4,128,128]{2,1,0:T(8,128)S(1)}, u32[]{:S(2)}, u32[]{:S(2)}) collective-permute-start(f32[4,128,128]{2,1,0:T(8,128)S(1)} %convolution_add_fusion.6), channel_id=1, source_target_pairs={{0,8},{8,16},{16,24},{24,32},{32,40},{40,48},{48,56},{56,64},{64,7... | collective-permute-start | bytes 786440 | tf_op jit(solution)/shard_map/while/body/eval_jaxpr/ppermute | solution.py:14
  360.1 9.8 %collective-permute-start = (f32[4,128,128]{2,1,0:T(8,128)S(1)}, f32[4,128,128]{2,1,0:T(8,128)S(1)}, u32[]{:S(2)}, u32[]{:S(2)}) collective-permute-start(f32[4,128,128]{2,1,0:T(8,128)S(1)} %convolution_add_fusion.6), channel_id=1, source_target_pairs={{0,8},{8,16},{16,24},{24,32},{32,40},{40,48},{48,56},{56,64},{64,7... | collective-permute-start | bytes 786440 | tf_op jit(solution)/shard_map/while/body/eval_jaxpr/ppermute | solution.py:14
  370.3 9.8 %collective-permute-start = (f32[4,128,128]{2,1,0:T(8,128)S(1)}, f32[4,128,128]{2,1,0:T(8,128)S(1)}, u32[]{:S(2)}, u32[]{:S(2)}) collective-permute-start(f32[4,128,128]{2,1,0:T(8,128)S(1)} %convolution_add_fusion.6), channel_id=1, source_target_pairs={{0,8},{8,16},{16,24},{24,32},{32,40},{40,48},{48,56},{56,64},{64,7... | collective-permute-start | bytes 786440 | tf_op jit(solution)/shard_map/while/body/eval_jaxpr/ppermute | solution.py:14
  380.6 9.8 %collective-permute-start = (f32[4,128,128]{2,1,0:T(8,128)S(1)}, f32[4,128,128]{2,1,0:T(8,128)S(1)}, u32[]{:S(2)}, u32[]{:S(2)}) collective-permute-start(f32[4,128,128]{2,1,0:T(8,128)S(1)} %convolution_add_fusion.6), channel_id=1, source_target_pairs={{0,8},{8,16},{16,24},{24,32},{32,40},{40,48},{48,56},{56,64},{64,7... | collective-permute-start | bytes 786440 | tf_op jit(solution)/shard_map/while/body/eval_jaxpr/ppermute | solution.py:14
  390.8 9.8 %collective-permute-start = (f32[4,128,128]{2,1,0:T(8,128)S(1)}, f32[4,128,128]{2,1,0:T(8,128)S(1)}, u32[]{:S(2)}, u32[]{:S(2)}) collective-permute-start(f32[4,128,128]{2,1,0:T(8,128)S(1)} %convolution_add_fusion.6), channel_id=1, source_target_pairs={{0,8},{8,16},{16,24},{24,32},{32,40},{40,48},{48,56},{56,64},{64,7... | collective-permute-start | bytes 786440 | tf_op jit(solution)/shard_map/while/body/eval_jaxpr/ppermute | solution.py:14
  401.1 9.8 %collective-permute-start = (f32[4,128,128]{2,1,0:T(8,128)S(1)}, f32[4,128,128]{2,1,0:T(8,128)S(1)}, u32[]{:S(2)}, u32[]{:S(2)}) collective-permute-start(f32[4,128,128]{2,1,0:T(8,128)S(1)} %convolution_add_fusion.6), channel_id=1, source_target_pairs={{0,8},{8,16},{16,24},{24,32},{32,40},{40,48},{48,56},{56,64},{64,7... | collective-permute-start | bytes 786440 | tf_op jit(solution)/shard_map/while/body/eval_jaxpr/ppermute | solution.py:14
  411.4 9.8 %collective-permute-start = (f32[4,128,128]{2,1,0:T(8,128)S(1)}, f32[4,128,128]{2,1,0:T(8,128)S(1)}, u32[]{:S(2)}, u32[]{:S(2)}) collective-permute-start(f32[4,128,128]{2,1,0:T(8,128)S(1)} %convolution_add_fusion.6), channel_id=1, source_target_pairs={{0,8},{8,16},{16,24},{24,32},{32,40},{40,48},{48,56},{56,64},{64,7... | collective-permute-start | bytes 786440 | tf_op jit(solution)/shard_map/while/body/eval_jaxpr/ppermute | solution.py:14
  421.6 9.8 %collective-permute-start = (f32[4,128,128]{2,1,0:T(8,128)S(1)}, f32[4,128,128]{2,1,0:T(8,128)S(1)}, u32[]{:S(2)}, u32[]{:S(2)}) collective-permute-start(f32[4,128,128]{2,1,0:T(8,128)S(1)} %convolution_add_fusion.6), channel_id=1, source_target_pairs={{0,8},{8,16},{16,24},{24,32},{32,40},{40,48},{48,56},{56,64},{64,7... | collective-permute-start | bytes 786440 | tf_op jit(solution)/shard_map/while/body/eval_jaxpr/ppermute | solution.py:14
  431.9 9.8 %collective-permute-start = (f32[4,128,128]{2,1,0:T(8,128)S(1)}, f32[4,128,128]{2,1,0:T(8,128)S(1)}, u32[]{:S(2)}, u32[]{:S(2)}) collective-permute-start(f32[4,128,128]{2,1,0:T(8,128)S(1)} %convolution_add_fusion.6), channel_id=1, source_target_pairs={{0,8},{8,16},{16,24},{24,32},{32,40},{40,48},{48,56},{56,64},{64,7... | collective-permute-start | bytes 786440 | tf_op jit(solution)/shard_map/while/body/eval_jaxpr/ppermute | solution.py:14
  442.1 9.8 %collective-permute-start = (f32[4,128,128]{2,1,0:T(8,128)S(1)}, f32[4,128,128]{2,1,0:T(8,128)S(1)}, u32[]{:S(2)}, u32[]{:S(2)}) collective-permute-start(f32[4,128,128]{2,1,0:T(8,128)S(1)} %convolution_add_fusion.6), channel_id=1, source_target_pairs={{0,8},{8,16},{16,24},{24,32},{32,40},{40,48},{48,56},{56,64},{64,7... | collective-permute-start | bytes 786440 | tf_op jit(solution)/shard_map/while/body/eval_jaxpr/ppermute | solution.py:14
  452.4 9.8 %collective-permute-start = (f32[4,128,128]{2,1,0:T(8,128)S(1)}, f32[4,128,128]{2,1,0:T(8,128)S(1)}, u32[]{:S(2)}, u32[]{:S(2)}) collective-permute-start(f32[4,128,128]{2,1,0:T(8,128)S(1)} %convolution_add_fusion.6), channel_id=1, source_target_pairs={{0,8},{8,16},{16,24},{24,32},{32,40},{40,48},{48,56},{56,64},{64,7... | collective-permute-start | bytes 786440 | tf_op jit(solution)/shard_map/while/body/eval_jaxpr/ppermute | solution.py:14
  462.6 9.8 %collective-permute-start = (f32[4,128,128]{2,1,0:T(8,128)S(1)}, f32[4,128,128]{2,1,0:T(8,128)S(1)}, u32[]{:S(2)}, u32[]{:S(2)}) collective-permute-start(f32[4,128,128]{2,1,0:T(8,128)S(1)} %convolution_add_fusion.6), channel_id=1, source_target_pairs={{0,8},{8,16},{16,24},{24,32},{32,40},{40,48},{48,56},{56,64},{64,7... | collective-permute-start | bytes 786440 | tf_op jit(solution)/shard_map/while/body/eval_jaxpr/ppermute | solution.py:14
  472.9 9.8 %collective-permute-start = (f32[4,128,128]{2,1,0:T(8,128)S(1)}, f32[4,128,128]{2,1,0:T(8,128)S(1)}, u32[]{:S(2)}, u32[]{:S(2)}) collective-permute-start(f32[4,128,128]{2,1,0:T(8,128)S(1)} %convolution_add_fusion.6), channel_id=1, source_target_pairs={{0,8},{8,16},{16,24},{24,32},{32,40},{40,48},{48,56},{56,64},{64,7... | collective-permute-start | bytes 786440 | tf_op jit(solution)/shard_map/while/body/eval_jaxpr/ppermute | solution.py:14
  483.1 9.8 %collective-permute-start = (f32[4,128,128]{2,1,0:T(8,128)S(1)}, f32[4,128,128]{2,1,0:T(8,128)S(1)}, u32[]{:S(2)}, u32[]{:S(2)}) collective-permute-start(f32[4,128,128]{2,1,0:T(8,128)S(1)} %convolution_add_fusion.6), channel_id=1, source_target_pairs={{0,8},{8,16},{16,24},{24,32},{32,40},{40,48},{48,56},{56,64},{64,7... | collective-permute-start | bytes 786440 | tf_op jit(solution)/shard_map/while/body/eval_jaxpr/ppermute | solution.py:14
  493.4 9.8 %collective-permute-start = (f32[4,128,128]{2,1,0:T(8,128)S(1)}, f32[4,128,128]{2,1,0:T(8,128)S(1)}, u32[]{:S(2)}, u32[]{:S(2)}) collective-permute-start(f32[4,128,128]{2,1,0:T(8,128)S(1)} %convolution_add_fusion.6), channel_id=1, source_target_pairs={{0,8},{8,16},{16,24},{24,32},{32,40},{40,48},{48,56},{56,64},{64,7... | collective-permute-start | bytes 786440 | tf_op jit(solution)/shard_map/while/body/eval_jaxpr/ppermute | solution.py:14
  503.6 9.8 %collective-permute-start = (f32[4,128,128]{2,1,0:T(8,128)S(1)}, f32[4,128,128]{2,1,0:T(8,128)S(1)}, u32[]{:S(2)}, u32[]{:S(2)}) collective-permute-start(f32[4,128,128]{2,1,0:T(8,128)S(1)} %convolution_add_fusion.6), channel_id=1, source_target_pairs={{0,8},{8,16},{16,24},{24,32},{32,40},{40,48},{48,56},{56,64},{64,7... | collective-permute-start | bytes 786440 | tf_op jit(solution)/shard_map/while/body/eval_jaxpr/ppermute | solution.py:14
  513.9 9.8 %collective-permute-start = (f32[4,128,128]{2,1,0:T(8,128)S(1)}, f32[4,128,128]{2,1,0:T(8,128)S(1)}, u32[]{:S(2)}, u32[]{:S(2)}) collective-permute-start(f32[4,128,128]{2,1,0:T(8,128)S(1)} %convolution_add_fusion.6), channel_id=1, source_target_pairs={{0,8},{8,16},{16,24},{24,32},{32,40},{40,48},{48,56},{56,64},{64,7... | collective-permute-start | bytes 786440 | tf_op jit(solution)/shard_map/while/body/eval_jaxpr/ppermute | solution.py:14
  524.1 9.8 %collective-permute-start = (f32[4,128,128]{2,1,0:T(8,128)S(1)}, f32[4,128,128]{2,1,0:T(8,128)S(1)}, u32[]{:S(2)}, u32[]{:S(2)}) collective-permute-start(f32[4,128,128]{2,1,0:T(8,128)S(1)} %convolution_add_fusion.6), channel_id=1, source_target_pairs={{0,8},{8,16},{16,24},{24,32},{32,40},{40,48},{48,56},{56,64},{64,7... | collective-permute-start | bytes 786440 | tf_op jit(solution)/shard_map/while/body/eval_jaxpr/ppermute | solution.py:14
  534.4 9.8 %collective-permute-start = (f32[4,128,128]{2,1,0:T(8,128)S(1)}, f32[4,128,128]{2,1,0:T(8,128)S(1)}, u32[]{:S(2)}, u32[]{:S(2)}) collective-permute-start(f32[4,128,128]{2,1,0:T(8,128)S(1)} %convolution_add_fusion.6), channel_id=1, source_target_pairs={{0,8},{8,16},{16,24},{24,32},{32,40},{40,48},{48,56},{56,64},{64,7... | collective-permute-start | bytes 786440 | tf_op jit(solution)/shard_map/while/body/eval_jaxpr/ppermute | solution.py:14
  544.6 9.8 %collective-permute-start = (f32[4,128,128]{2,1,0:T(8,128)S(1)}, f32[4,128,128]{2,1,0:T(8,128)S(1)}, u32[]{:S(2)}, u32[]{:S(2)}) collective-permute-start(f32[4,128,128]{2,1,0:T(8,128)S(1)} %convolution_add_fusion.6), channel_id=1, source_target_pairs={{0,8},{8,16},{16,24},{24,32},{32,40},{40,48},{48,56},{56,64},{64,7... | collective-permute-start | bytes 786440 | tf_op jit(solution)/shard_map/while/body/eval_jaxpr/ppermute | solution.py:14
  554.9 9.8 %collective-permute-start = (f32[4,128,128]{2,1,0:T(8,128)S(1)}, f32[4,128,128]{2,1,0:T(8,128)S(1)}, u32[]{:S(2)}, u32[]{:S(2)}) collective-permute-start(f32[4,128,128]{2,1,0:T(8,128)S(1)} %convolution_add_fusion.6), channel_id=1, source_target_pairs={{0,8},{8,16},{16,24},{24,32},{32,40},{40,48},{48,56},{56,64},{64,7... | collective-permute-start | bytes 786440 | tf_op jit(solution)/shard_map/while/body/eval_jaxpr/ppermute | solution.py:14
  565.2 9.8 %collective-permute-start = (f32[4,128,128]{2,1,0:T(8,128)S(1)}, f32[4,128,128]{2,1,0:T(8,128)S(1)}, u32[]{:S(2)}, u32[]{:S(2)}) collective-permute-start(f32[4,128,128]{2,1,0:T(8,128)S(1)} %convolution_add_fusion.6), channel_id=1, source_target_pairs={{0,8},{8,16},{16,24},{24,32},{32,40},{40,48},{48,56},{56,64},{64,7... | collective-permute-start | bytes 786440 | tf_op jit(solution)/shard_map/while/body/eval_jaxpr/ppermute | solution.py:14
  575.4 9.8 %collective-permute-start = (f32[4,128,128]{2,1,0:T(8,128)S(1)}, f32[4,128,128]{2,1,0:T(8,128)S(1)}, u32[]{:S(2)}, u32[]{:S(2)}) collective-permute-start(f32[4,128,128]{2,1,0:T(8,128)S(1)} %convolution_add_fusion.6), channel_id=1, source_target_pairs={{0,8},{8,16},{16,24},{24,32},{32,40},{40,48},{48,56},{56,64},{64,7... | collective-permute-start | bytes 786440 | tf_op jit(solution)/shard_map/while/body/eval_jaxpr/ppermute | solution.py:14
  585.7 9.8 %collective-permute-start = (f32[4,128,128]{2,1,0:T(8,128)S(1)}, f32[4,128,128]{2,1,0:T(8,128)S(1)}, u32[]{:S(2)}, u32[]{:S(2)}) collective-permute-start(f32[4,128,128]{2,1,0:T(8,128)S(1)} %convolution_add_fusion.6), channel_id=1, source_target_pairs={{0,8},{8,16},{16,24},{24,32},{32,40},{40,48},{48,56},{56,64},{64,7... | collective-permute-start | bytes 786440 | tf_op jit(solution)/shard_map/while/body/eval_jaxpr/ppermute | solution.py:14
  595.9 9.8 %collective-permute-start = (f32[4,128,128]{2,1,0:T(8,128)S(1)}, f32[4,128,128]{2,1,0:T(8,128)S(1)}, u32[]{:S(2)}, u32[]{:S(2)}) collective-permute-start(f32[4,128,128]{2,1,0:T(8,128)S(1)} %convolution_add_fusion.6), channel_id=1, source_target_pairs={{0,8},{8,16},{16,24},{24,32},{32,40},{40,48},{48,56},{56,64},{64,7... | collective-permute-start | bytes 786440 | tf_op jit(solution)/shard_map/while/body/eval_jaxpr/ppermute | solution.py:14
Sparse Core Ops, SparseCore 0:
  9.7 46.4 all-gather.1
where the time goes:
time: 626 us; the launch traced here: 618 us
  waiting for transfers between devices  275 us (44%)
  other arithmetic  180 us (29%)
  starting transfers between devices  73.3 us (12%)
  matrix products  61.3 us (10%)
  between operations  14.4 us (2%)
  local copies, waits for them, and re-layouts  12.3 us (2%)
    ppermute x32, waiting for transfers between devices, passed_along(): return lax.ppermute(block, axis, route)  235 us
    another operation x4, other arithmetic, body(): jax.scipy.linalg.solve_triangular(system, right_side, lower=True, unit_di...  159 us
    ppermute x32, starting transfers between devices, passed_along(): return lax.ppermute(block, axis, route)  73.2 us
    all_gather x1, waiting for transfers between devices, body(): piece = lax.all_gather(hidden, 'head', axis=1, tiled=True)  39.5 us
    dot_general x48, matrix products, matmul_heads(): jnp.einsum('hij,hjk->hik', left, right, precision=lax.Precision.HIGHEST)  38.3 us
  transfers between devices with their start and end apart: 33, of which 33 were waited for; matrix products, arithmetic and copies ran while one was open for 1% of the time, Pallas kernels for 0%

commit v1 on v0

v1 whole, which is shorter than its diff:
```python
import functools

import jax
import jax.numpy as jnp
from jax import lax
from jax.experimental import pallas as pl
from jax.experimental.pallas import tpu as pltpu
from jax.sharding import PartitionSpec as P

MESH = pl.DeviceIdType.MESH
F32 = jnp.float32
BF16 = jnp.bfloat16
SUB = 128
HALO = 16
LEVELS = (2, 4, 8, 16, 32, 64)
NT = (((1,), (1,)), ((), ()))


def mm(left, right):
    return jnp.dot(left, right, preferred_element_type=F32)


def mm_nt(left, right):
    return lax.dot_general(left, right, NT, preferred_element_type=F32)


def split3(value):
    high = value.astype(BF16).astype(F32)
    mid = (value - high).astype(BF16).astype(F32)
    low = value - high - mid
    row = lax.broadcasted_iota(jnp.int32, (16, SUB), 0)
    tile = jnp.where(row == 0, high, jnp.where(row == 1, mid, jnp.where(row == 2, low, 0.0)))
    return tile.astype(BF16)


def joined3(tile):
    return jnp.sum(tile.astype(F32), axis=0, keepdims=True)


def kernel(
    n_seq,
    n_head,
    hidden_ref,
    wq_ref,
    wk_ref,
    wv_ref,
    cq_ref,
    ck_ref,
    cv_ref,
    gate_hbm,
    beta_hbm,
    init_hbm,
    core_ref,
    closing_ref,
    gbuf,
    own_halo,
    w_ref,
    gate_ref,
    beta_ref,
    init_ref,
    x_ref,
    tap_ref,
    mask_ref,
    state_ref,
    decay_ref,
    partial_ref,
    reach_ref,
    total_ref,
    tx0,
    rx0,
    tx1,
    rx1,
    tx2,
    inc_ref,
    initt_ref,
    local_sem,
    ring_send,
    ring_recv,
    halo_sem,
    pair_sem,
    a_send,
    a_recv,
    b_send,
    b_recv,
):
    tokens = hidden_ref.shape[0]
    width = hidden_ref.shape[1]
    blocks = tokens // SUB
    heads = gate_hbm.shape[0]
    qcols = wq_ref.shape[1]
    n_chip = n_seq // 2
    me_s = lax.axis_index("seq")
    me_h = lax.axis_index("head")
    core = lax.rem(me_s, 2)
    chip = lax.div(me_s, 2)
    partner = me_s + 1 - 2 * core
    right = lax.rem(me_h + 1, n_head)
    left = lax.rem(me_h + n_head - 1, n_head)

    own_halo[...] = jnp.zeros_like(own_halo)
    barrier = pltpu.get_barrier_semaphore()
    for neighbour in (left, right):
        pl.semaphore_signal(
            barrier, inc=1, device_id={"seq": me_s, "head": neighbour}, device_id_type=MESH
        )

    def greet(i, carry):
        @pl.when(i != me_s)
        def _():
            pl.semaphore_signal(
                barrier, inc=1, device_id={"seq": i, "head": me_h}, device_id_type=MESH
            )

        return carry

    lax.fori_loop(0, n_seq, greet, 0)

    loads = []
    for source, target in (
        (wq_ref, w_ref.at[:, pl.ds(0, qcols)]),
        (wk_ref, w_ref.at[:, pl.ds(qcols, qcols)]),
        (wv_ref, w_ref.at[:, pl.ds(2 * qcols, wv_ref.shape[1])]),
        (gate_hbm, gate_ref),
        (beta_hbm, beta_ref),
        (init_hbm, init_ref),
    ):
        loads.append(pltpu.make_async_copy(source, target, local_sem.at[1 + len(loads)]))
        loads[-1].start()

    row = lax.broadcasted_iota(jnp.int32, (SUB, SUB), 0)
    col = lax.broadcasted_iota(jnp.int32, (SUB, SUB), 1)
    for index, size in enumerate(LEVELS):
        here = (lax.div(row, 2 * size) == lax.div(col, 2 * size)) & (
            lax.div(row, size) > lax.div(col, size)
        )
        mask_ref[index] = jnp.where(here, 1.0, 0.0).astype(BF16)
    tap_ref[:, :qcols] = cq_ref[...].astype(F32)
    tap_ref[:, qcols : 2 * qcols] = ck_ref[...].astype(F32)
    tap_ref[:, 2 * qcols :] = cv_ref[...].astype(F32)
    state_ref[...] = jnp.zeros_like(state_ref)
    decay_ref[...] = jnp.ones_like(decay_ref)

    pl.semaphore_wait(barrier, n_seq - 1 + 2)

    halo_copy = pltpu.make_async_remote_copy(
        src_ref=hidden_ref.at[pl.ds(tokens - HALO, HALO)],
        dst_ref=own_halo,
        send_sem=halo_sem.at[0],
        recv_sem=halo_sem.at[1],
        device_id={"seq": lax.rem(me_s + 1, n_seq), "head": me_h},
        device_id_type=MESH,
    )

    @pl.when(me_s < n_seq - 1)
    def _():
        halo_copy.start()

    half = n_head // 2
    part_rows = SUB // 2

    def hop(direction, chunk, part, distance):
        back = distance - 1
        if direction == 0:
            owner, target = lax.rem(me_h + n_head - back, n_head), right
        else:
            owner, target = lax.rem(me_h + back, n_head), left
        if isinstance(chunk, int) and chunk == blocks:
            rows = pl.ds(tokens, HALO)
        else:
            rows = pl.ds(pl.multiple_of(chunk * SUB + part * part_rows, part_rows), part_rows)
        columns = pl.ds(pl.multiple_of(owner * width, width), width)
        place = gbuf.at[rows, columns]
        if distance > 1:
            source = place
        elif isinstance(chunk, int) and chunk == blocks:
            source = own_halo
        else:
            source = hidden_ref.at[rows]
        return pltpu.make_async_remote_copy(
            src_ref=source,
            dst_ref=place,
            send_sem=ring_send.at[direction, chunk, part, back],
            recv_sem=ring_recv.at[direction, chunk, part, back],
            device_id={"seq": me_s, "head": target},
            device_id_type=MESH,
        )

    def used(direction, part, distance):
        return distance < half or (distance == half and part == direction)

    def event(chunk, part, distance):
        for direction in (0, 1):
            if used(direction, part, distance):
                if distance > 1:
                    hop(direction, chunk, part, distance - 1).wait_recv()
                hop(direction, chunk, part, distance).start()

    def arrived(chunk, parts=(0, 1)):
        for part in parts:
            for direction in (0, 1):
                last = half if used(direction, part, half) else half - 1
                if last:
                    hop(direction, chunk, part, last).wait_recv()

    def sent(chunk, parts=(0, 1)):
        for part in parts:
            for direction in (0, 1):
                for distance in range(1, half + 1):
                    if used(direction, part, distance):
                        hop(direction, chunk, part, distance).wait_send()

    split = max(half // 2, 1)
    early, late = range(1, split + 1), range(split + 1, half + 1)

    def ring_events(chunk):
        calls = []
        for k in range(max(len(early), len(late))):
            for part in (0, 1):
                if k < len(late):
                    calls.append((0, part, late[k]))
                if k < len(early):
                    calls.append((1, part, early[k]))

        def make(ahead, part, distance):
            def call():
                @pl.when(chunk + ahead < blocks)
                def _():
                    event(chunk + ahead, part, distance)

            return call

        return [make(*call) for call in calls]

    own_columns = pl.ds(pl.multiple_of(me_h * width, width), width)
    own_copy = pltpu.make_async_copy(
        hidden_ref, gbuf.at[pl.ds(0, tokens), own_columns], local_sem.at[0]
    )
    own_copy.start()
    for distance in early:
        for part in (0, 1):
            event(0, part, distance)

    @pl.when(me_s > 0)
    def _():
        halo_copy.wait_recv()

    gbuf[pl.ds(tokens, HALO), own_columns] = own_halo[...]
    calls = ring_events(0)
    event(blocks, 0, 1)
    for index, call in enumerate(calls):
        call()
        if index % 2 == 1 and index // 2 + 2 <= half:
            event(blocks, 0, index // 2 + 2)
    own_copy.wait()
    for copy in loads:
        copy.wait()
    arrived(blocks, (0,))

    def project(start, size, place, columns=slice(None)):
        rows = gbuf[pl.ds(start, size), :]
        x_ref[pl.ds(place, size), columns] = mm(rows, w_ref[:, columns]).astype(BF16).astype(F32)

    project(tokens, HALO, 0)

    def conv(base, columns):
        total = None
        window = x_ref[pl.ds(base, SUB + HALO), columns]
        for tap in range(4):
            first = HALO - 3 + tap
            term = tap_ref[tap : tap + 1, columns] * window[first : first + SUB]
            total = term if total is None else total + term
        return (total / (1.0 + jnp.exp(-total))).astype(BF16)

    def unit(value, factor):
        value = value.astype(F32)
        squares = jnp.sum(value * value, axis=1, keepdims=True)
        return (value * (lax.rsqrt(squares + 1e-06) * factor)).astype(BF16)

    def block_step(n, carry):
        base = pl.multiple_of(n * SUB, SUB)
        here = pl.ds(base, SUB)
        calls = ring_events(n + 1)

        def service(count=1):
            for _ in range(min(count, len(calls))):
                calls.pop(0)()

        arrived(n)
        for part in range(2):
            service()
            columns = slice(part * 2 * qcols, part * 2 * qcols + 2 * qcols)
            project(base, SUB, pl.multiple_of(base + HALO, HALO), columns)
        service()
        on_or_below = row >= col
        below = row > col
        gates = gate_ref[:, here]
        betas = beta_ref[:, here]
        along = jnp.dot(
            jnp.concatenate([gates, gates], axis=0),
            jnp.where(row <= col, 1.0, 0.0),
            precision=lax.Precision.HIGHEST,
            preferred_element_type=F32,
        )[:heads]
        columns8 = jnp.concatenate([along, betas], axis=0).T
        keys, queries, grams, mixes = [], [], [], []
        for kh in range(qcols // SUB):
            at = slice(SUB * kh, SUB * kh + SUB)
            q = unit(conv(base, at), SUB**-0.5)
            k = unit(conv(base, slice(qcols + SUB * kh, qcols + SUB * kh + SUB)), 1.0)
            both = mm_nt(jnp.concatenate([k, q], axis=0), k)
            keys.append(k)
            queries.append(q.astype(F32))
            grams.append(both[:SUB])
            mixes.append(both[SUB:])
        service()
        keys_t = [k.astype(F32).T for k in keys]
        per_key = heads // len(keys)
        lowers, solved, query_mixes, rights = [], [], [], []
        for h in range(heads):
            kh = h // per_key
            c_col = columns8[:, h : h + 1]
            b_col = columns8[:, heads + h : heads + h + 1]
            spread = c_col - along[h : h + 1, :]
            decay = jnp.exp(jnp.where(on_or_below, spread, -1e30))
            lower = jnp.where(below, decay * grams[kh], 0.0) * b_col
            lowers.append(lower.astype(BF16))
            query_mixes.append((decay * mixes[kh]).astype(BF16))
            first = jnp.where(lax.div(row, 2) == lax.div(col, 2), lower, 0.0)
            solved.append((jnp.where(row == col, 1.0, 0.0) - first).astype(BF16))
            v = conv(base, slice(2 * qcols + SUB * h, 2 * qcols + SUB * h + SUB))
            rights.append(
                jnp.concatenate(
                    [
                        (b_col * v.astype(F32)).astype(BF16),
                        ((b_col * jnp.exp(c_col)) * keys[kh].astype(F32)).astype(BF16),
                    ],
                    axis=1,
                )
            )
        for index in range(len(LEVELS)):
            if index % 2 == 0:
                service()
            halves = [
                mm(t, low * mask_ref[index]).astype(BF16) for t, low in zip(solved, lowers)
            ]
            solved = [t - mm(x, t).astype(BF16) for t, x in zip(solved, halves)]
        service(len(calls))
        updates = [mm(t, r).astype(BF16) for t, r in zip(solved, rights)]
        stacked = []
        for h in range(heads):
            to_end = jnp.exp(along[h : h + 1, SUB - 1 :] - along[h : h + 1, :])
            weighted = (keys_t[h // per_key] * to_end).astype(BF16)
            stacked.append(
                mm(jnp.concatenate([query_mixes[h], weighted], axis=0), updates[h])
            )
        for h in range(heads):
            both = stacked[h]
            retain = jnp.exp(columns8[:, h : h + 1])
            keep = jnp.exp(along[h : h + 1, SUB - 1 :])
            query_eff = retain * queries[h // per_key] - both[:SUB, SUB:]
            offset, correction = both[SUB:, :SUB], both[SUB:, SUB:]
            state = state_ref[h]
            so_far = decay_ref[h, 0:1, 0:1]
            moved = mm(
                jnp.concatenate([query_eff, correction], axis=0).astype(BF16),
                state.astype(BF16),
            )
            at = slice(SUB * h, SUB * h + SUB)
            partial_ref[here, at] = both[:SUB, :SUB] + moved[:SUB, :SUB]
            reach_ref[here, at] = (so_far * query_eff - moved[:SUB, SUB:]).astype(BF16)
            state_ref[h, :, :SUB] = keep * state[:, :SUB] - moved[SUB:, :SUB] + offset
            state_ref[h, :, SUB:] = (
                keep * state[:, SUB:] + so_far * correction - moved[SUB:, SUB:]
            )
            decay_ref[h] = decay_ref[h] * keep
        return carry

    lax.fori_loop(0, blocks, block_step, 0)

    for h in range(heads):
        total_ref[h, :SUB] = state_ref[h, :, SUB:].T
        total_ref[h, SUB:] = state_ref[h, :, :SUB].T
        tx0[h, :SUB] = total_ref[h, :SUB].astype(BF16)
        tx0[h, SUB : SUB + 16] = split3(decay_ref[h, 0:1, :])
        tx0[h, SUB + 16 :] = total_ref[h, SUB:].astype(BF16)
    pair = pltpu.make_async_remote_copy(
        src_ref=tx0,
        dst_ref=rx0,
        send_sem=pair_sem.at[0],
        recv_sem=pair_sem.at[1],
        device_id={"seq": partner, "head": me_h},
        device_id_type=MESH,
    )
    pair.start()
    pair.wait()

    own_heads = heads // 2
    slices = n_chip // heads
    slab = SUB // slices
    for i in range(own_heads):
        h = core * own_heads + i
        mine, other = tx0[h], rx0[h]
        flag = (jnp.zeros((1, 1), jnp.int32) + core) == 0
        early = jnp.where(flag, mine.astype(F32), other.astype(F32))
        late = jnp.where(flag, other.astype(F32), mine.astype(F32))
        g0 = joined3(early[SUB : SUB + 16])
        g1 = joined3(late[SUB : SUB + 16])
        c0, s0 = early[:SUB], early[SUB + 16 :]
        c1, s1 = late[:SUB], late[SUB + 16 :]
        moved = mm(jnp.concatenate([c0, s0], axis=0).astype(BF16), c1.astype(BF16))
        c_new = (g1 * c0 + g0 * c1 - moved[:SUB]).astype(BF16)
        s_new = (g1 * s0 + s1 - moved[SUB:]).astype(BF16)
        g_new = split3(g0 * g1)
        for part in range(slices):
            tx1[i, part, :SUB] = c_new
            tx1[i, part, SUB : SUB + 16] = g_new
            tx1[i, part, SUB + 16 :] = s_new[slab * part : slab * part + slab]

    def job(q):
        part = lax.div(q, heads)
        head = lax.rem(part + q, heads)
        return part, head

    def to_handler(q):
        part, head = job(q)
        return pltpu.make_async_remote_copy(
            src_ref=tx1.at[lax.rem(head, own_heads), part],
            dst_ref=rx1.at[chip],
            send_sem=a_send.at[q],
            recv_sem=a_recv.at[chip],
            device_id={"seq": 2 * q + core, "head": me_h},
            device_id_type=MESH,
        )

    def for_me(q):
        return lax.div(job(q)[1], own_heads) == core

    def send_a(q, carry):
        @pl.when((q != chip) & for_me(q))
        def _():
            to_handler(q).start()

        return carry

    lax.fori_loop(0, n_chip, send_a, 0)
    my_part, my_head = job(chip)
    handling = for_me(chip)

    def from_handler(q):
        part, head = job(q)
        return inc_ref.at[head, pl.ds(pl.multiple_of(part * slab, slab), slab)]

    def hand_on(i, other_core):
        return pltpu.make_async_remote_copy(
            src_ref=tx2.at[i],
            dst_ref=from_handler(chip),
            send_sem=b_send.at[i, other_core],
            recv_sem=b_recv.at[chip],
            device_id={"seq": 2 * i + other_core, "head": me_h},
            device_id_type=MESH,
        )

    @pl.when(handling)
    def _():
        rx1[chip] = tx1[lax.rem(my_head, own_heads), my_part]
        initt_ref[...] = init_ref[my_head].T
        state0 = initt_ref[pl.ds(pl.multiple_of(my_part * slab, slab), slab)]

        def chain(i, state):
            tx2[i] = state
            for other_core in (0, 1):

                @pl.when(2 * i + other_core != me_s)
                def _():
                    hand_on(i, other_core).start()

            @pl.when(i != chip)
            def _():
                pltpu.make_async_remote_copy(
                    src_ref=tx1.at[0, 0],
                    dst_ref=rx1.at[i],
                    send_sem=a_send.at[i],
                    recv_sem=a_recv.at[i],
                    device_id={"seq": partner, "head": me_h},
                    device_id_type=MESH,
                ).wait_recv()

            message = rx1[i]
            moved = mm(state.astype(BF16), message[:SUB])
            keep = joined3(message[SUB : SUB + 16])
            return keep * state - moved + message[SUB + 16 :].astype(F32)

        lax.fori_loop(0, n_chip, chain, state0)
        inc_ref[my_head, pl.ds(pl.multiple_of(my_part * slab, slab), slab)] = tx2[chip]

    def receive(q, carry):
        @pl.when(2 * q + lax.div(job(q)[1], own_heads) != me_s)
        def _():
            pltpu.make_async_remote_copy(
                src_ref=tx2.at[0],
                dst_ref=from_handler(q),
                send_sem=b_send.at[0, 0],
                recv_sem=b_recv.at[q],
                device_id={"seq": partner, "head": me_h},
                device_id_type=MESH,
            ).wait_recv()

        return carry

    lax.fori_loop(0, n_chip, receive, 0)

    for h in range(heads):
        came = inc_ref[h]
        first = rx0[h]
        stepped = (
            joined3(first[SUB : SUB + 16]) * came
            - mm(came.astype(BF16), first[:SUB])
            + first[SUB + 16 :].astype(F32)
        )
        flag = (jnp.zeros((1, 1), jnp.int32) + core) == 0
        came = jnp.where(flag, came, stepped)
        at = slice(SUB * h, SUB * h + SUB)
        short = came.astype(BF16)
        core_ref[:, at] = (partial_ref[:, at] + mm_nt(reach_ref[:, at], short)).astype(BF16)
        total = total_ref[h]
        closing = (
            decay_ref[h, 0:1, :] * came - mm(short, total[:SUB].astype(BF16)) + total[SUB:]
        )
        closing_ref[0, h] = closing.T

    @pl.when(me_s < n_seq - 1)
    def _():
        halo_copy.wait_send()

    def sent_ring(chunk, carry):
        sent(chunk)
        return carry

    lax.fori_loop(0, blocks, sent_ring, 0)
    sent(blocks, (0,))

    def sent_a(q, carry):
        @pl.when((q != chip) & for_me(q))
        def _():
            to_handler(q).wait_send()

        return carry

    lax.fori_loop(0, n_chip, sent_a, 0)

    @pl.when(handling)
    def _():
        def sent_b(i, carry):
            for other_core in (0, 1):

                @pl.when(2 * i + other_core != me_s)
                def _():
                    hand_on(i, other_core).wait_send()

            return carry

        lax.fori_loop(0, n_chip, sent_b, 0)


def solution(mesh):
    n_seq, n_head = mesh.shape["seq"], mesh.shape["head"]
    n_chip = n_seq // 2

    def body(hidden, wq, wk, wv, cq, ck, cv, gate, beta, init):
        tokens, width = hidden.shape
        heads = gate.shape[0]
        columns = wq.shape[1] + wk.shape[1] + wv.shape[1]
        slices = n_chip // heads
        slab = SUB // slices
        blocks = tokens // SUB
        vmem = pl.BlockSpec(memory_space=pltpu.VMEM)
        hbm = pl.BlockSpec(memory_space=pltpu.HBM)
        dma = pltpu.SemaphoreType.DMA
        return pl.pallas_call(
            functools.partial(kernel, n_seq, n_head),
            out_shape=(
                jax.ShapeDtypeStruct((tokens, wv.shape[1]), BF16),
                jax.ShapeDtypeStruct((1,) + init.shape, F32),
            ),
            in_specs=[hbm] * 4 + [vmem] * 3 + [hbm] * 3,
            out_specs=(vmem, vmem),
            scratch_shapes=[
                pltpu.VMEM((tokens + HALO, width * n_head), BF16),
                pltpu.VMEM((HALO, width), BF16),
                pltpu.VMEM((wq.shape[0], columns), BF16),
                pltpu.VMEM(gate.shape, F32),
                pltpu.VMEM(beta.shape, F32),
                pltpu.VMEM(init.shape, F32),
                pltpu.VMEM((tokens + HALO, columns), F32),
                pltpu.VMEM((4, columns), F32),
                pltpu.VMEM((len(LEVELS), SUB, SUB), BF16),
                pltpu.VMEM((heads, SUB, 2 * SUB), F32),
                pltpu.VMEM((heads, 8, SUB), F32),
                pltpu.VMEM((tokens, wv.shape[1]), F32),
                pltpu.VMEM((tokens, wv.shape[1]), BF16),
                pltpu.VMEM((heads, 2 * SUB, SUB), F32),
                pltpu.VMEM((heads, 2 * SUB + 16, SUB), BF16),
                pltpu.VMEM((heads, 2 * SUB + 16, SUB), BF16),
                pltpu.VMEM((heads // 2, slices, SUB + 16 + slab, SUB), BF16),
                pltpu.VMEM((n_chip, SUB + 16 + slab, SUB), BF16),
                pltpu.VMEM((n_chip, slab, SUB), F32),
                pltpu.VMEM((heads, SUB, SUB), F32),
                pltpu.VMEM((SUB, SUB), F32),
                dma((7,)),
                dma((2, blocks + 1, 2, n_head // 2)),
                dma((2, blocks + 1, 2, n_head // 2)),
                dma((2,)),
                dma((2,)),
                dma((n_chip,)),
                dma((n_chip,)),
                dma((n_chip, 2)),
                dma((n_chip,)),
            ],
            compiler_params=pltpu.CompilerParams(
                collective_id=0, has_side_effects=True, vmem_limit_bytes=48 * 2**20
            ),
        )(hidden, wq, wk, wv, cq, ck, cv, gate, beta, init)

    return jax.shard_map(
        body,
        mesh=mesh,
        in_specs=(
            P("seq", "head"),
            P(None, "head"),
            P(None, "head"),
            P(None, "head"),
            P(None, "head"),
            P(None, "head"),
            P(None, "head"),
            P("head", "seq"),
            P("head", "seq"),
            P("head", None, None),
        ),
        out_specs=(P("seq", "head"), P("seq", "head", None, None)),
        check_vma=False,
    )
```

time: 626 us -> 84.7 us (0.14); the launches traced: 618 us -> 83.8 us
  waiting for transfers between devices: 275 us -> 0 us
  other arithmetic: 180 us -> 0 us
  starting transfers between devices: 73.3 us -> 0 us
  Pallas kernels: 0 us -> 72.3 us
  matrix products: 61.3 us -> 0 us
  between operations: 14.4 us -> 0.66 us
    ppermute x32 -> x0, waiting for transfers between devices: 235 us -> none  [passed_along(): return lax.ppermute(block, axis, route)]
    another operation x7 -> x0, other arithmetic: 162 us -> none  [the longest x4 159 us: body(): jax.scipy.linalg.solve_triangular(system, right_side, lower=True, unit_di...]
    ppermute x32 -> x0, starting transfers between devices: 73.2 us -> none  [passed_along(): return lax.ppermute(block, axis, route)]
    pallas_call x0 -> x1, Pallas kernels: none -> 72.3 us  [body(): pl.pallas_call(functools.partial(kernel, n_seq, n_head), out_shape=(jax.S...]
    dot_general x58 -> x0, matrix products: 59.3 us -> none  [the longest x48 38.3 us: matmul_heads(): jnp.einsum('hij,hjk->hik', left, right, precision=lax.Precision.HIGHEST)]
    all_gather x1 -> x0, waiting for transfers between devices: 39.5 us -> none  [body(): piece = lax.all_gather(hidden, 'head', axis=1, tiled=True)]
    unnamed x29 -> x22, local copies, waits for them, and re-layouts: 2.3 us -> 10.9 us
    mul x5 -> x0, other arithmetic: 7.3 us -> none  [the longest x3 4.29 us: conv_silu(): kernel[tap_index].astype(jnp.float32)]
  transfers between devices with their start and end apart: 33 -> 0, of which waited for: 33 -> 0; matrix products, arithmetic and copies ran while one was open for 1% -> 0% of each run, Pallas kernels for 0% -> 0%
where the time goes in v1:
time: 84.7 us; the launch traced here: 83.8 us
  Pallas kernels  72.3 us (85%)
  local copies, waits for them, and re-layouts  10.9 us (13%)
    pallas_call x1, Pallas kernels, body(): pl.pallas_call(functools.partial(kernel, n_seq, n_head), out_shape=(jax.S...  72.3 us
    unnamed x22, local copies, waits for them, and re-layouts  10.9 us

profile of v1, /device:TPU:7, one launch (start us, length us, event | category | flops | bytes accessed | tf_op | source)
XLA Modules:
  0.0 83.8 jit_solution(1568324257516585800)
XLA Ops:
  0.6 0.0 copy-start
  0.6 1.6 %copy-done = bf16[2048,512]{1,0:T(8,128)(2,1)S(1)} copy-done((bf16[2048,512]{1,0:T(8,128)(2,1)S(1)}, bf16[2048,512]{1,0:T(8,128)(2,1)}, u32[]{:S(2)}) %copy-start) | copy-done | bytes 2097176
  2.2 0.0 copy-start.1
  2.2 1.2 %copy-done.1 = bf16[2048,256]{1,0:T(8,128)(2,1)S(1)} copy-done((bf16[2048,256]{1,0:T(8,128)(2,1)S(1)}, bf16[2048,256]{1,0:T(8,128)(2,1)}, u32[]{:S(2)}) %copy-start.1) | copy-done | bytes 1048600
  3.5 0.0 copy-start.2
  3.5 1.2 %copy-done.2 = bf16[2048,256]{1,0:T(8,128)(2,1)S(1)} copy-done((bf16[2048,256]{1,0:T(8,128)(2,1)S(1)}, bf16[2048,256]{1,0:T(8,128)(2,1)}, u32[]{:S(2)}) %copy-start.2) | copy-done | bytes 1048600
  4.7 0.0 copy-start.3
  4.7 0.9 %copy-done.3 = bf16[512,256]{1,0:T(8,128)(2,1)S(1)} copy-done((bf16[512,256]{1,0:T(8,128)(2,1)S(1)}, bf16[512,256]{1,0:T(8,128)(2,1)}, u32[]{:S(2)}) %copy-start.3) | copy-done | bytes 262168
  5.6 0.0 copy-start.4
  5.6 0.9 %copy-done.4 = f32[4,128,128]{2,1,0:T(8,128)S(1)} copy-done((f32[4,128,128]{2,1,0:T(8,128)S(1)}, f32[4,128,128]{2,1,0:T(8,128)}, u32[]{:S(2)}) %copy-start.4) | copy-done | bytes 262168
  6.6 0.0 copy-start.5
  6.6 0.7 copy-done.5
  7.3 0.0 copy-start.6
  7.3 0.7 copy-done.6
  8.0 0.0 copy-start.7
  8.0 0.7 copy-done.7
  8.7 0.0 copy-start.8
  8.7 0.7 copy-done.8
  9.3 0.0 copy-start.9
  9.3 0.7 copy-done.9
  10.0 72.3 %shard_map.113 = (bf16[512,512]{1,0:T(8,128)(2,1)S(1)}, f32[1,4,128,128]{3,2,1,0:T(8,128)S(1)}) custom-call(bf16[512,256]{1,0:T(8,128)(2,1)S(1)} %copy-done.3, bf16[2048,256]{1,0:T(8,128)(2,1)S(1)} %copy-done.1, bf16[2048,256]{1,0:T(8,128)(2,1)S(1)} %copy-done.2, bf16[2048,512]{1,0:T(8,128)(2,1)S(1)} %copy-done, bf16[4,256]{1,0:T(4,128)(2,1)S(1)} %copy-done.8, ...), custom_call_target="tpu_custom_call" | custom-call | tf_op jit(solution)/shard_map/pallas_call | solution.py:579
  82.4 0.8 copy.14
  83.1 0.7 copy.15
Async XLA Ops:
  0.6 1.6 %copy-start = (bf16[2048,512]{1,0:T(8,128)(2,1)S(1)}, bf16[2048,512]{1,0:T(8,128)(2,1)}, u32[]{:S(2)}) copy-start(bf16[2048,512]{1,0:T(8,128)(2,1)} %wv_ref.1) | copy-start | bytes 6291460
  2.2 1.2 %copy-start.1 = (bf16[2048,256]{1,0:T(8,128)(2,1)S(1)}, bf16[2048,256]{1,0:T(8,128)(2,1)}, u32[]{:S(2)}) copy-start(bf16[2048,256]{1,0:T(8,128)(2,1)} %wq_ref.1) | copy-start | bytes 3145732
  3.5 1.2 %copy-start.2 = (bf16[2048,256]{1,0:T(8,128)(2,1)S(1)}, bf16[2048,256]{1,0:T(8,128)(2,1)}, u32[]{:S(2)}) copy-start(bf16[2048,256]{1,0:T(8,128)(2,1)} %wk_ref.1) | copy-start | bytes 3145732
  4.7 0.9 %copy-start.3 = (bf16[512,256]{1,0:T(8,128)(2,1)S(1)}, bf16[512,256]{1,0:T(8,128)(2,1)}, u32[]{:S(2)}) copy-start(bf16[512,256]{1,0:T(8,128)(2,1)} %hidden_ref.1) | copy-start | bytes 786436
  5.6 0.9 %copy-start.4 = (f32[4,128,128]{2,1,0:T(8,128)S(1)}, f32[4,128,128]{2,1,0:T(8,128)}, u32[]{:S(2)}) copy-start(f32[4,128,128]{2,1,0:T(8,128)} %init_hbm.1) | copy-start | bytes 786436
  6.6 0.7 copy-start.5
  7.3 0.7 copy-start.6
  8.0 0.7 copy-start.7
  8.7 0.7 copy-start.8
  9.3 0.7 copy-start.9

commit v2 on v1

v2 whole, which is shorter than its diff:
```python
import functools

import jax
import jax.numpy as jnp
from jax import lax
from jax.experimental import pallas as pl
from jax.experimental.pallas import tpu as pltpu
from jax.sharding import PartitionSpec as P

MESH = pl.DeviceIdType.MESH
F32 = jnp.float32
BF16 = jnp.bfloat16
SUB = 128
HALO = 16
LEVELS = (2, 4, 8, 16, 32, 64)
FIRST = (
    (0, 0, 0), (1, 1, 0), (1, 0, 0), (2, 0, 0), (0, 1, 0), (0, 0, 1), (1, 1, 1),
    (1, 0, 1), (3, 0, 0), (0, 1, 1), (0, 0, 2), (3, 1, 0), (1, 0, 2), (2, 0, 1),
    (3, 0, 1), (0, 1, 2), (2, 1, 0), (0, 0, 3), (1, 1, 2), (1, 0, 3), (2, 0, 2),
    (2, 1, 1), (3, 0, 2), (3, 1, 1),
)
BESIDE = ((4, 2, 0, 3), (5, 2, 1, 2), (6, 3, 0, 3), (7, 3, 1, 2))
NT = (((1,), (1,)), ((), ()))


def mm(left, right):
    return jnp.dot(left, right, preferred_element_type=F32)


def mm_nt(left, right):
    return lax.dot_general(left, right, NT, preferred_element_type=F32)


def split3(value):
    high = value.astype(BF16).astype(F32)
    mid = (value - high).astype(BF16).astype(F32)
    low = value - high - mid
    row = lax.broadcasted_iota(jnp.int32, (16, SUB), 0)
    tile = jnp.where(row == 0, high, jnp.where(row == 1, mid, jnp.where(row == 2, low, 0.0)))
    return tile.astype(BF16)


def joined3(tile):
    return jnp.sum(tile.astype(F32), axis=0, keepdims=True)


def kernel(
    n_seq,
    n_head,
    hidden_ref,
    wq_ref,
    wk_ref,
    wv_ref,
    cq_hbm,
    ck_hbm,
    cv_hbm,
    gate_hbm,
    beta_hbm,
    init_hbm,
    core_ref,
    closing_ref,
    gbuf,
    w_ref,
    gate_ref,
    beta_ref,
    init_ref,
    cq_ref,
    ck_ref,
    cv_ref,
    x_ref,
    tap_ref,
    mask_ref,
    state_ref,
    decay_ref,
    decays_ref,
    factor_ref,
    retain_ref,
    beta_full,
    both_full,
    rows_ref,
    partial_ref,
    reach_ref,
    total_ref,
    tx0,
    rx0,
    tx1,
    rx1,
    tx2,
    inc_ref,
    initt_ref,
    local_sem,
    sent_sem,
    ring_recv,
    halo_sem,
    pair_sem,
    a_recv,
    b_recv,
):
    tokens = hidden_ref.shape[0]
    width = hidden_ref.shape[1]
    blocks = tokens // SUB
    heads = gate_hbm.shape[0]
    qcols = wq_ref.shape[1]
    n_chip = n_seq // 2
    me_s = lax.axis_index("seq")
    me_h = lax.axis_index("head")
    core = lax.rem(me_s, 2)
    chip = lax.div(me_s, 2)
    partner = me_s + 1 - 2 * core
    right = lax.rem(me_h + 1, n_head)
    left = lax.rem(me_h + n_head - 1, n_head)

    barrier = pltpu.get_barrier_semaphore()
    for neighbour in (left, right):
        pl.semaphore_signal(
            barrier, inc=1, device_id={"seq": me_s, "head": neighbour}, device_id_type=MESH
        )
    later = lax.rem(me_s + 1, n_seq)
    sooner = lax.rem(me_s + n_seq - 1, n_seq)
    for step in range(1, n_head):
        for other in (later, sooner):
            pl.semaphore_signal(
                barrier,
                inc=1,
                device_id={"seq": other, "head": lax.rem(me_h + step, n_head)},
                device_id_type=MESH,
            )

    def greet(i, carry):
        @pl.when(i != me_s)
        def _():
            pl.semaphore_signal(
                barrier, inc=1, device_id={"seq": i, "head": me_h}, device_id_type=MESH
            )

        return carry

    lax.fori_loop(0, n_seq, greet, 0)

    own_columns = pl.ds(pl.multiple_of(me_h * width, width), width)
    own_copy = pltpu.make_async_copy(
        hidden_ref, gbuf.at[pl.ds(0, tokens), own_columns], local_sem.at[0]
    )
    own_copy.start()
    loads = []
    for source, target in (
        (wq_ref, w_ref.at[:, pl.ds(0, qcols)]),
        (wk_ref, w_ref.at[:, pl.ds(qcols, qcols)]),
        (wv_ref, w_ref.at[:, pl.ds(2 * qcols, wv_ref.shape[1])]),
        (gate_hbm, gate_ref),
        (beta_hbm, beta_ref),
        (init_hbm, init_ref),
        (cq_hbm, cq_ref),
        (ck_hbm, ck_ref),
        (cv_hbm, cv_ref),
    ):
        loads.append(pltpu.make_async_copy(source, target, local_sem.at[1 + len(loads)]))
        loads[-1].start()

    row = lax.broadcasted_iota(jnp.int32, (SUB, SUB), 0)
    col = lax.broadcasted_iota(jnp.int32, (SUB, SUB), 1)
    for index, size in enumerate(LEVELS):
        here = (lax.div(row, 2 * size) == lax.div(col, 2 * size)) & (
            lax.div(row, size) > lax.div(col, size)
        )
        mask_ref[index] = jnp.where(here, 1.0, 0.0).astype(BF16)
    state_ref[...] = jnp.zeros_like(state_ref)
    decay_ref[...] = jnp.ones_like(decay_ref)

    own_copy.wait()
    pl.semaphore_wait(barrier, n_seq - 1 + 2 + 2 * (n_head - 1))

    part_rows = SUB // 2

    def hop(way, chunk, which, back):
        owner = lax.rem(me_h + (n_head - back if way == 0 else back), n_head)
        part = way + which - 2 * way * which
        rows = pl.ds(pl.multiple_of(chunk * SUB + part * part_rows, part_rows), part_rows)
        place = gbuf.at[rows, pl.ds(pl.multiple_of(owner * width, width), width)]
        return pltpu.make_async_remote_copy(
            src_ref=place,
            dst_ref=place,
            send_sem=sent_sem.at[0],
            recv_sem=ring_recv.at[way, 2 * chunk + which, back],
            device_id={"seq": me_s, "head": right if way == 0 else left},
            device_id_type=MESH,
        )

    def event(chunk, which, back):
        for way in (0, 1):
            if isinstance(back, int):
                if back:
                    hop(way, chunk, which, back - 1).wait_recv()
            else:

                @pl.when(back > 0)
                def _():
                    hop(way, chunk, which, back - 1).wait_recv()

            hop(way, chunk, which, back).start()

    def service(pair, stage):
        entries = [entry[1:] for entry in BESIDE if entry[0] == stage]
        if entries:

            @pl.when(pair == 0)
            def _():
                for entry in entries:
                    event(*entry)

    def arrived(chunk):
        for way in (0, 1):
            hop(way, chunk, 0, 3).wait_recv()
            hop(way, chunk, 1, 2).wait_recv()

    def halo_hop(step):
        return pltpu.make_async_remote_copy(
            src_ref=gbuf.at[pl.ds(tokens - HALO, HALO), own_columns],
            dst_ref=gbuf.at[pl.ds(tokens, HALO), own_columns],
            send_sem=sent_sem.at[1],
            recv_sem=halo_sem.at[0],
            device_id={"seq": later, "head": lax.rem(me_h + step, n_head)},
            device_id_type=MESH,
        )

    on_or_below = row >= col
    below = row > col

    def prepare(n):
        at = slice(SUB * n, SUB * n + SUB)
        gates = gate_ref[:, at]
        along = jnp.dot(
            jnp.concatenate([gates, gates], axis=0),
            jnp.where(row <= col, 1.0, 0.0),
            precision=lax.Precision.HIGHEST,
            preferred_element_type=F32,
        )[:heads]
        columns8 = jnp.concatenate([along, beta_ref[:, at]], axis=0).T
        for h in range(heads):
            index = n * heads + h
            c_row, c_end = along[h : h + 1, :], along[h : h + 1, SUB - 1 :]
            c_col = columns8[:, h : h + 1]
            b_col = columns8[:, heads + h : heads + h + 1]
            retain = jnp.exp(c_col)
            decay = jnp.exp(jnp.where(on_or_below, c_col - c_row, -1e30))
            decays_ref[index] = decay
            factor_ref[index] = jnp.where(below, decay, 0.0) * b_col
            retain_ref[index] = jnp.broadcast_to(retain, (SUB, SUB))
            beta_full[index] = jnp.broadcast_to(b_col, (SUB, SUB))
            both_full[index] = jnp.broadcast_to(b_col * retain, (SUB, SUB))
            rows_ref[index, 0:1] = jnp.exp(c_end - c_row)
            rows_ref[index, 1:2] = jnp.broadcast_to(jnp.exp(c_end), (1, SUB))

    halo_bytes = gbuf.at[pl.ds(tokens, HALO)]

    def project(start, size, place, columns=slice(None)):
        rows = gbuf[pl.ds(start, size), :]
        x_ref[pl.ds(place, size), columns] = mm(rows, w_ref[:, columns]).astype(BF16).astype(F32)

    def start_conv():
        tap_ref[:, :qcols] = cq_ref[...].astype(F32)
        tap_ref[:, qcols : 2 * qcols] = ck_ref[...].astype(F32)
        tap_ref[:, 2 * qcols :] = cv_ref[...].astype(F32)
        pltpu.make_async_copy(halo_bytes, halo_bytes, halo_sem.at[0]).wait()
        project(tokens, HALO, 0)

        @pl.when(me_s == 0)
        def _():
            x_ref[:HALO] = jnp.zeros((HALO, x_ref.shape[1]), F32)

    for entry in FIRST[:2]:
        event(*entry)
    for step in range(n_head):
        halo_hop(step).start()
    for copy in loads:
        copy.wait()
    for index, entry in enumerate(FIRST[2:], 2):
        if index in (5, 9, 12, 15):
            prepare((5, 9, 12, 15).index(index))
        if index == 17:
            start_conv()
        event(*entry)
    def conv(base, columns):
        total = None
        window = x_ref[pl.ds(base, SUB + HALO), columns]
        for tap in range(4):
            first = HALO - 3 + tap
            term = tap_ref[tap : tap + 1, columns] * window[first : first + SUB]
            total = term if total is None else total + term
        return (total / (1.0 + jnp.exp(-total))).astype(BF16)

    def unit(value, factor):
        value = value.astype(F32)
        squares = jnp.sum(value * value, axis=1, keepdims=True)
        return (value * (lax.rsqrt(squares + 1e-06) * factor)).astype(BF16)

    per_key = heads // (qcols // SUB)

    def project_block(pair, stage, n):
        base = pl.multiple_of(n * SUB, SUB)
        arrived(n)
        for part in range(2):
            service(pair, stage + part)
            columns = slice(part * 2 * qcols, part * 2 * qcols + 2 * qcols)
            project(base, SUB, pl.multiple_of(base + HALO, HALO), columns)

    def systems(n):
        base = pl.multiple_of(n * SUB, SUB)
        found = []
        for kh in range(qcols // SUB):
            at = slice(SUB * kh, SUB * kh + SUB)
            q = unit(conv(base, at), SUB**-0.5)
            k = unit(conv(base, slice(qcols + SUB * kh, qcols + SUB * kh + SUB)), 1.0)
            both = mm_nt(jnp.concatenate([k, q], axis=0), k)
            k = k.astype(F32)
            k_t = k.T
            for h in range(per_key * kh, per_key * kh + per_key):
                index = n * heads + h
                lower = factor_ref[index] * both[:SUB]
                mix = (decays_ref[index] * both[SUB:]).astype(BF16)
                first = jnp.where(lax.div(row, 2) == lax.div(col, 2), lower, 0.0)
                start = (jnp.where(row == col, 1.0, 0.0) - first).astype(BF16)
                v = conv(base, slice(2 * qcols + SUB * h, 2 * qcols + SUB * h + SUB))
                right_side = jnp.concatenate(
                    [
                        (beta_full[index] * v.astype(F32)).astype(BF16),
                        (both_full[index] * k).astype(BF16),
                    ],
                    axis=1,
                )
                weighted = (k_t * rows_ref[index, 0:1]).astype(BF16)
                query = retain_ref[index] * q.astype(F32)
                found.append(
                    (
                        lower.astype(BF16),
                        start,
                        right_side,
                        jnp.concatenate([mix, weighted], axis=0),
                        query,
                    )
                )
        return found

    def pair_step(pair, carry):
        found = []
        for n in (2 * pair, 2 * pair + 1):
            stage = 3 * (len(found) // heads)
            project_block(pair, stage, n)
            service(pair, stage + 2)
            found += systems(n)
        lowers = [each[0] for each in found]
        solved = [each[1] for each in found]
        for index in range(len(LEVELS)):
            if index % 2 == 0:
                service(pair, 6 + index // 2)
            halves = [
                mm(t, low * mask_ref[index]).astype(BF16) for t, low in zip(solved, lowers)
            ]
            solved = [t - mm(x, t).astype(BF16) for t, x in zip(solved, halves)]
        updates = [mm(t, each[2]).astype(BF16) for t, each in zip(solved, found)]
        stacked = [mm(each[3], u) for u, each in zip(updates, found)]
        for second in range(2):
            n = 2 * pair + second
            here = pl.ds(pl.multiple_of(n * SUB, SUB), SUB)
            for h in range(heads):
                both = stacked[heads * second + h]
                keep = rows_ref[n * heads + h, 1:2]
                query_eff = found[heads * second + h][4] - both[:SUB, SUB:]
                offset, correction = both[SUB:, :SUB], both[SUB:, SUB:]
                state = state_ref[h]
                so_far = decay_ref[h, 0:1]
                moved = mm(
                    jnp.concatenate([query_eff, correction], axis=0).astype(BF16),
                    state.astype(BF16),
                )
                at = slice(SUB * h, SUB * h + SUB)
                partial_ref[here, at] = both[:SUB, :SUB] + moved[:SUB, :SUB]
                reach_ref[here, at] = (so_far * query_eff - moved[:SUB, SUB:]).astype(BF16)
                state_ref[h, :, :SUB] = keep * state[:, :SUB] - moved[SUB:, :SUB] + offset
                state_ref[h, :, SUB:] = (
                    keep * state[:, SUB:] + so_far * correction - moved[SUB:, SUB:]
                )
                decay_ref[h] = decay_ref[h] * keep
        return carry

    lax.fori_loop(0, blocks // 2, pair_step, 0)

    for h in range(heads):
        total_ref[h, :SUB] = state_ref[h, :, SUB:].T
        total_ref[h, SUB:] = state_ref[h, :, :SUB].T
        tx0[h, :SUB] = total_ref[h, :SUB].astype(BF16)
        tx0[h, SUB : SUB + 16] = split3(decay_ref[h, 0:1, :])
        tx0[h, SUB + 16 :] = total_ref[h, SUB:].astype(BF16)
    pair = pltpu.make_async_remote_copy(
        src_ref=tx0,
        dst_ref=rx0,
        send_sem=pair_sem.at[0],
        recv_sem=pair_sem.at[1],
        device_id={"seq": partner, "head": me_h},
        device_id_type=MESH,
    )
    pair.start()
    pair.wait()

    own_heads = heads // 2
    slices = n_chip // heads
    slab = SUB // slices
    for i in range(own_heads):
        h = core * own_heads + i
        mine, other = tx0[h], rx0[h]
        flag = (jnp.zeros((1, 1), jnp.int32) + core) == 0
        early = jnp.where(flag, mine.astype(F32), other.astype(F32))
        late = jnp.where(flag, other.astype(F32), mine.astype(F32))
        g0 = joined3(early[SUB : SUB + 16])
        g1 = joined3(late[SUB : SUB + 16])
        c0, s0 = early[:SUB], early[SUB + 16 :]
        c1, s1 = late[:SUB], late[SUB + 16 :]
        moved = mm(jnp.concatenate([c0, s0], axis=0).astype(BF16), c1.astype(BF16))
        c_new = (g1 * c0 + g0 * c1 - moved[:SUB]).astype(BF16)
        s_new = (g1 * s0 + s1 - moved[SUB:]).astype(BF16)
        g_new = split3(g0 * g1)
        for part in range(slices):
            tx1[i, part, :SUB] = c_new
            tx1[i, part, SUB : SUB + 16] = g_new
            tx1[i, part, SUB + 16 :] = s_new[slab * part : slab * part + slab]

    def job(q):
        part = lax.div(q, heads)
        head = lax.rem(part + q, heads)
        return part, head

    def to_handler(q):
        part, head = job(q)
        return pltpu.make_async_remote_copy(
            src_ref=tx1.at[lax.rem(head, own_heads), part],
            dst_ref=rx1.at[chip],
            send_sem=sent_sem.at[2],
            recv_sem=a_recv.at[chip],
            device_id={"seq": 2 * q + core, "head": me_h},
            device_id_type=MESH,
        )

    def for_me(q):
        return lax.div(job(q)[1], own_heads) == core

    def send_a(k, carry):
        q = chip ^ k

        @pl.when((q != chip) & for_me(q))
        def _():
            to_handler(q).start()

        return carry

    lax.fori_loop(0, n_chip, send_a, 0)
    my_part, my_head = job(chip)
    handling = for_me(chip)

    def from_handler(q):
        part, head = job(q)
        return inc_ref.at[head, pl.ds(pl.multiple_of(part * slab, slab), slab)]

    def hand_on(i, other_core):
        return pltpu.make_async_remote_copy(
            src_ref=tx2.at[i],
            dst_ref=from_handler(chip),
            send_sem=sent_sem.at[3],
            recv_sem=b_recv.at[0],
            device_id={"seq": 2 * i + other_core, "head": me_h},
            device_id_type=MESH,
        )

    @pl.when(handling)
    def _():
        rx1[chip] = tx1[lax.rem(my_head, own_heads), my_part]
        initt_ref[...] = init_ref[my_head].T
        state0 = initt_ref[pl.ds(pl.multiple_of(my_part * slab, slab), slab)]

        def chain(i, state):
            tx2[i] = state
            for other_core in (0, 1):

                @pl.when(2 * i + other_core != me_s)
                def _():
                    hand_on(i, other_core).start()

            @pl.when(i != chip)
            def _():
                pltpu.make_async_remote_copy(
                    src_ref=tx1.at[0, 0],
                    dst_ref=rx1.at[i],
                    send_sem=sent_sem.at[2],
                    recv_sem=a_recv.at[i],
                    device_id={"seq": partner, "head": me_h},
                    device_id_type=MESH,
                ).wait_recv()

            message = rx1[i]
            moved = mm(state.astype(BF16), message[:SUB])
            keep = joined3(message[SUB : SUB + 16])
            return keep * state - moved + message[SUB + 16 :].astype(F32)

        lax.fori_loop(0, n_chip, chain, state0)
        inc_ref[my_head, pl.ds(pl.multiple_of(my_part * slab, slab), slab)] = tx2[chip]

    @pl.when(handling)
    def _():
        b_bytes = partial_ref.at[pl.ds(0, (n_chip - 1) * slab // 2), pl.ds(0, 2 * SUB)]
        pltpu.make_async_copy(b_bytes, b_bytes, b_recv.at[0]).wait()

    @pl.when(jnp.logical_not(handling))
    def _():
        b_bytes = partial_ref.at[pl.ds(0, n_chip * slab // 2), pl.ds(0, 2 * SUB)]
        pltpu.make_async_copy(b_bytes, b_bytes, b_recv.at[0]).wait()

    for h in range(heads):
        came = inc_ref[h]
        first = rx0[h]
        stepped = (
            joined3(first[SUB : SUB + 16]) * came
            - mm(came.astype(BF16), first[:SUB])
            + first[SUB + 16 :].astype(F32)
        )
        flag = (jnp.zeros((1, 1), jnp.int32) + core) == 0
        came = jnp.where(flag, came, stepped)
        at = slice(SUB * h, SUB * h + SUB)
        short = came.astype(BF16)
        core_ref[:, at] = (partial_ref[:, at] + mm_nt(reach_ref[:, at], short)).astype(BF16)
        total = total_ref[h]
        closing = (
            decay_ref[h, 0:1, :] * came - mm(short, total[:SUB].astype(BF16)) + total[SUB:]
        )
        closing_ref[0, h] = closing.T

    ring_bytes = gbuf.at[pl.ds(0, tokens), pl.ds(0, (n_head - 1) * width)]
    pltpu.make_async_copy(ring_bytes, ring_bytes, sent_sem.at[0]).wait()
    pltpu.make_async_copy(halo_bytes, halo_bytes, sent_sem.at[1]).wait()

    messages = n_chip // 2

    @pl.when(handling)
    def _():
        a_bytes = rx1.at[pl.ds(0, messages - 1)]
        pltpu.make_async_copy(a_bytes, a_bytes, sent_sem.at[2]).wait()
        b_bytes = partial_ref.at[pl.ds(0, (n_seq - 1) * slab // 2), pl.ds(0, 2 * SUB)]
        pltpu.make_async_copy(b_bytes, b_bytes, sent_sem.at[3]).wait()

    @pl.when(jnp.logical_not(handling))
    def _():
        a_bytes = rx1.at[pl.ds(0, messages)]
        pltpu.make_async_copy(a_bytes, a_bytes, sent_sem.at[2]).wait()


def solution(mesh):
    n_seq, n_head = mesh.shape["seq"], mesh.shape["head"]
    n_chip = n_seq // 2

    def body(hidden, wq, wk, wv, cq, ck, cv, gate, beta, init):
        tokens, width = hidden.shape
        heads = gate.shape[0]
        columns = wq.shape[1] + wk.shape[1] + wv.shape[1]
        slices = n_chip // heads
        slab = SUB // slices
        blocks = tokens // SUB
        vmem = pl.BlockSpec(memory_space=pltpu.VMEM)
        hbm = pl.BlockSpec(memory_space=pltpu.HBM)
        dma = pltpu.SemaphoreType.DMA
        return pl.pallas_call(
            functools.partial(kernel, n_seq, n_head),
            out_shape=(
                jax.ShapeDtypeStruct((tokens, wv.shape[1]), BF16),
                jax.ShapeDtypeStruct((1,) + init.shape, F32),
            ),
            in_specs=[hbm] * 10,
            out_specs=(vmem, vmem),
            scratch_shapes=[
                pltpu.VMEM((tokens + HALO, width * n_head), BF16),
                pltpu.VMEM((wq.shape[0], columns), BF16),
                pltpu.VMEM(gate.shape, F32),
                pltpu.VMEM(beta.shape, F32),
                pltpu.VMEM(init.shape, F32),
                pltpu.VMEM(cq.shape, BF16),
                pltpu.VMEM(ck.shape, BF16),
                pltpu.VMEM(cv.shape, BF16),
                pltpu.VMEM((tokens + HALO, columns), F32),
                pltpu.VMEM((4, columns), F32),
                pltpu.VMEM((len(LEVELS), SUB, SUB), BF16),
                pltpu.VMEM((heads, SUB, 2 * SUB), F32),
                pltpu.VMEM((heads, 8, SUB), F32),
                pltpu.VMEM((blocks * heads, SUB, SUB), F32),
                pltpu.VMEM((blocks * heads, SUB, SUB), F32),
                pltpu.VMEM((blocks * heads, SUB, SUB), F32),
                pltpu.VMEM((blocks * heads, SUB, SUB), F32),
                pltpu.VMEM((blocks * heads, SUB, SUB), F32),
                pltpu.VMEM((blocks * heads, 8, SUB), F32),
                pltpu.VMEM((tokens, wv.shape[1]), F32),
                pltpu.VMEM((tokens, wv.shape[1]), BF16),
                pltpu.VMEM((heads, 2 * SUB, SUB), F32),
                pltpu.VMEM((heads, 2 * SUB + 16, SUB), BF16),
                pltpu.VMEM((heads, 2 * SUB + 16, SUB), BF16),
                pltpu.VMEM((heads // 2, slices, SUB + 16 + slab, SUB), BF16),
                pltpu.VMEM((n_chip, SUB + 16 + slab, SUB), BF16),
                pltpu.VMEM((n_chip, slab, SUB), F32),
                pltpu.VMEM((heads, SUB, SUB), F32),
                pltpu.VMEM((SUB, SUB), F32),
                dma((10,)),
                dma((4,)),
                dma((2, 2 * blocks, n_head // 2)),
                dma((1,)),
                dma((2,)),
                dma((n_chip,)),
                dma((1,)),
            ],
            compiler_params=pltpu.CompilerParams(
                collective_id=0, has_side_effects=True, vmem_limit_bytes=60 * 2**20
            ),
        )(hidden, wq, wk, wv, cq, ck, cv, gate, beta, init)

    return jax.shard_map(
        body,
        mesh=mesh,
        in_specs=(
            P("seq", "head"),
            P(None, "head"),
            P(None, "head"),
            P(None, "head"),
            P(None, "head"),
            P(None, "head"),
            P(None, "head"),
            P("head", "seq"),
            P("head", "seq"),
            P("head", None, None),
        ),
        out_specs=(P("seq", "head"), P("seq", "head", None, None)),
        check_vma=False,
    )
```

time: 84.7 us -> 61 us (0.72)
  Pallas kernels: 72.3 us -> 56.6 us
  local copies, waits for them, and re-layouts: 10.9 us -> 3.54 us
    pallas_call x1, Pallas kernels: 72.3 us -> 56.6 us  [body(): pl.pallas_call(functools.partial(kernel, n_seq, n_head), out_shape=(jax.S...]
    unnamed x22 -> x2, local copies, waits for them, and re-layouts: 10.9 us -> 3.54 us
where the time goes in v2:
time: 61 us; the launch traced here: 60.8 us
  Pallas kernels  56.6 us (93%)
  local copies, waits for them, and re-layouts  3.54 us (6%)
  between operations  0.64 us (1%)
    pallas_call x1, Pallas kernels, body(): pl.pallas_call(functools.partial(kernel, n_seq, n_head), out_shape=(jax.S...  56.6 us
    unnamed x2, local copies, waits for them, and re-layouts  3.54 us

profile of v2, /device:TPU:7, one launch (start us, length us, event | category | flops | bytes accessed | tf_op | source)
XLA Modules:
  0.0 60.8 jit_solution(137226379429801567)
XLA Ops:
  0.6 56.6 %shard_map.113 = (bf16[512,512]{1,0:T(8,128)(2,1)}, f32[1,4,128,128]{3,2,1,0:T(8,128)}) custom-call(bf16[512,256]{1,0:T(8,128)(2,1)} %hidden_ref.1, bf16[2048,256]{1,0:T(8,128)(2,1)} %wq_ref.1, bf16[2048,256]{1,0:T(8,128)(2,1)} %wk_ref.1, bf16[2048,512]{1,0:T(8,128)(2,1)} %wv_ref.1, bf16[4,256]{1,0:T(4,128)(2,1)} %cq_hbm.1, bf16[4,256]{1,0:T(4,128)(2,1)} %ck_hbm.1, ...), custom_call_target="tpu_custom_call" | custom-call | tf_op jit(solution)/shard_map/pallas_call | solution.py:568
  57.3 1.9 %copy.14 = bf16[512,512]{1,0:T(8,128)(2,1)} copy(bf16[512,512]{1,0:T(8,128)(2,1)} %get-tuple-element.4) | data formatting | bytes 1048576
  59.1 1.7 %copy.15 = f32[1,4,128,128]{3,2,1,0:T(8,128)} copy(f32[1,4,128,128]{3,2,1,0:T(8,128)} %get-tuple-element.5) | data formatting | bytes 524288

commit v3 on v2

--- a/solution.py
+++ b/solution.py
@@ -20,6 +20,7 @@
     (2, 1, 1), (3, 0, 2), (3, 1, 1),
 )
 BESIDE = ((4, 2, 0, 3), (5, 2, 1, 2), (6, 3, 0, 3), (7, 3, 1, 2))
+HALO_AFTER = (5, 10, 15, 20)
 NT = (((1,), (1,)), ((), ()))
 
 
@@ -116,15 +117,6 @@
             barrier, inc=1, device_id={"seq": me_s, "head": neighbour}, device_id_type=MESH
         )
     later = lax.rem(me_s + 1, n_seq)
-    sooner = lax.rem(me_s + n_seq - 1, n_seq)
-    for step in range(1, n_head):
-        for other in (later, sooner):
-            pl.semaphore_signal(
-                barrier,
-                inc=1,
-                device_id={"seq": other, "head": lax.rem(me_h + step, n_head)},
-                device_id_type=MESH,
-            )
 
     def greet(i, carry):
         @pl.when(i != me_s)
@@ -164,11 +156,14 @@
             lax.div(row, size) > lax.div(col, size)
         )
         mask_ref[index] = jnp.where(here, 1.0, 0.0).astype(BF16)
+    pairs = (lax.div(row, 2) == lax.div(col, 2)) & (row > col)
+    mask_ref[len(LEVELS)] = jnp.where(pairs, 1.0, 0.0).astype(BF16)
+    mask_ref[len(LEVELS) + 1] = jnp.where(row == col, 1.0, 0.0).astype(BF16)
     state_ref[...] = jnp.zeros_like(state_ref)
     decay_ref[...] = jnp.ones_like(decay_ref)
 
     own_copy.wait()
-    pl.semaphore_wait(barrier, n_seq - 1 + 2 + 2 * (n_head - 1))
+    pl.semaphore_wait(barrier, n_seq - 1 + 2)
 
     part_rows = SUB // 2
 
@@ -203,8 +198,7 @@
         entries = [entry[1:] for entry in BESIDE if entry[0] == stage]
         if entries:
 
-            @pl.when(pair == 0)
-            def _():
+            if pair == 0:
                 for entry in entries:
                     event(*entry)
 
@@ -213,15 +207,37 @@
             hop(way, chunk, 0, 3).wait_recv()
             hop(way, chunk, 1, 2).wait_recv()
 
-    def halo_hop(step):
+    halo_first = pltpu.make_async_remote_copy(
+        src_ref=gbuf.at[pl.ds(tokens - HALO, HALO), own_columns],
+        dst_ref=gbuf.at[pl.ds(tokens, HALO), own_columns],
+        send_sem=sent_sem.at[1],
+        recv_sem=halo_sem.at[0, n_head // 2],
+        device_id={"seq": later, "head": me_h},
+        device_id_type=MESH,
+    )
+
+    def halo_hop(way, back):
+        owner = lax.rem(me_h + (n_head - back if way == 0 else back), n_head)
+        place = gbuf.at[
+            pl.ds(tokens, HALO), pl.ds(pl.multiple_of(owner * width, width), width)
+        ]
         return pltpu.make_async_remote_copy(
-            src_ref=gbuf.at[pl.ds(tokens - HALO, HALO), own_columns],
-            dst_ref=gbuf.at[pl.ds(tokens, HALO), own_columns],
+            src_ref=place,
+            dst_ref=place,
             send_sem=sent_sem.at[1],
-            recv_sem=halo_sem.at[0],
-            device_id={"seq": later, "head": lax.rem(me_h + step, n_head)},
+            recv_sem=halo_sem.at[way, back],
+            device_id={"seq": me_s, "head": right if way == 0 else left},
             device_id_type=MESH,
         )
+
+    def halo_event(back):
+        if back == 0:
+            halo_first.wait_recv()
+        for way in (0, 1):
+            if back:
+                halo_hop(way, back - 1).wait_recv()
+            if back < n_head // 2 - way:
+                halo_hop(way, back).start()
 
     on_or_below = row >= col
     below = row > col
@@ -261,7 +277,7 @@
         tap_ref[:, :qcols] = cq_ref[...].astype(F32)
         tap_ref[:, qcols : 2 * qcols] = ck_ref[...].astype(F32)
         tap_ref[:, 2 * qcols :] = cv_ref[...].astype(F32)
-        pltpu.make_async_copy(halo_bytes, halo_bytes, halo_sem.at[0]).wait()
+        halo_hop(0, n_head // 2 - 1).wait_recv()
         project(tokens, HALO, 0)
 
         @pl.when(me_s == 0)
@@ -270,16 +286,15 @@
 
     for entry in FIRST[:2]:
         event(*entry)
-    for step in range(n_head):
-        halo_hop(step).start()
+    halo_first.start()
     for copy in loads:
         copy.wait()
     for index, entry in enumerate(FIRST[2:], 2):
         if index in (5, 9, 12, 15):
             prepare((5, 9, 12, 15).index(index))
-        if index == 17:
-            start_conv()
         event(*entry)
+        if index in HALO_AFTER:
+            halo_event(HALO_AFTER.index(index))
     def conv(base, columns):
         total = None
         window = x_ref[pl.ds(base, SUB + HALO), columns]
@@ -287,7 +302,7 @@
             first = HALO - 3 + tap
             term = tap_ref[tap : tap + 1, columns] * window[first : first + SUB]
             total = term if total is None else total + term
-        return (total / (1.0 + jnp.exp(-total))).astype(BF16)
+        return (total * pl.reciprocal(1.0 + jnp.exp(-total), approx=True)).astype(BF16)
 
     def unit(value, factor):
         value = value.astype(F32)
@@ -297,29 +312,29 @@
     per_key = heads // (qcols // SUB)
 
     def project_block(pair, stage, n):
-        base = pl.multiple_of(n * SUB, SUB)
+        base = n * SUB
         arrived(n)
         for part in range(2):
             service(pair, stage + part)
             columns = slice(part * 2 * qcols, part * 2 * qcols + 2 * qcols)
-            project(base, SUB, pl.multiple_of(base + HALO, HALO), columns)
+            project(base, SUB, base + HALO, columns)
 
     def systems(n):
-        base = pl.multiple_of(n * SUB, SUB)
+        base = n * SUB
         found = []
         for kh in range(qcols // SUB):
             at = slice(SUB * kh, SUB * kh + SUB)
             q = unit(conv(base, at), SUB**-0.5)
             k = unit(conv(base, slice(qcols + SUB * kh, qcols + SUB * kh + SUB)), 1.0)
-            both = mm_nt(jnp.concatenate([k, q], axis=0), k)
+            both = mm_nt(jnp.concatenate([k, q, mask_ref[len(LEVELS) + 1]], axis=0), k)
             k = k.astype(F32)
-            k_t = k.T
+            k_t = both[2 * SUB :]
             for h in range(per_key * kh, per_key * kh + per_key):
                 index = n * heads + h
                 lower = factor_ref[index] * both[:SUB]
-                mix = (decays_ref[index] * both[SUB:]).astype(BF16)
-                first = jnp.where(lax.div(row, 2) == lax.div(col, 2), lower, 0.0)
-                start = (jnp.where(row == col, 1.0, 0.0) - first).astype(BF16)
+                mix = (decays_ref[index] * both[SUB : 2 * SUB]).astype(BF16)
+                lower = lower.astype(BF16)
+                start = mask_ref[len(LEVELS) + 1] - lower * mask_ref[len(LEVELS)]
                 v = conv(base, slice(2 * qcols + SUB * h, 2 * qcols + SUB * h + SUB))
                 right_side = jnp.concatenate(
                     [
@@ -332,7 +347,7 @@
                 query = retain_ref[index] * q.astype(F32)
                 found.append(
                     (
-                        lower.astype(BF16),
+                        lower,
                         start,
                         right_side,
                         jnp.concatenate([mix, weighted], axis=0),
@@ -346,6 +361,8 @@
         for n in (2 * pair, 2 * pair + 1):
             stage = 3 * (len(found) // heads)
             project_block(pair, stage, n)
+            if stage == 0 and pair == 0:
+                start_conv()
             service(pair, stage + 2)
             found += systems(n)
         lowers = [each[0] for each in found]
@@ -361,7 +378,7 @@
         stacked = [mm(each[3], u) for u, each in zip(updates, found)]
         for second in range(2):
             n = 2 * pair + second
-            here = pl.ds(pl.multiple_of(n * SUB, SUB), SUB)
+            here = pl.ds(n * SUB, SUB)
             for h in range(heads):
                 both = stacked[heads * second + h]
                 keep = rows_ref[n * heads + h, 1:2]
@@ -383,7 +400,8 @@
                 decay_ref[h] = decay_ref[h] * keep
         return carry
 
-    lax.fori_loop(0, blocks // 2, pair_step, 0)
+    for pair in range(blocks // 2):
+        pair_step(pair, 0)
 
     for h in range(heads):
         total_ref[h, :SUB] = state_ref[h, :, SUB:].T
@@ -391,18 +409,23 @@
         tx0[h, :SUB] = total_ref[h, :SUB].astype(BF16)
         tx0[h, SUB : SUB + 16] = split3(decay_ref[h, 0:1, :])
         tx0[h, SUB + 16 :] = total_ref[h, SUB:].astype(BF16)
-    pair = pltpu.make_async_remote_copy(
-        src_ref=tx0,
-        dst_ref=rx0,
-        send_sem=pair_sem.at[0],
-        recv_sem=pair_sem.at[1],
-        device_id={"seq": partner, "head": me_h},
-        device_id_type=MESH,
-    )
-    pair.start()
-    pair.wait()
-
     own_heads = heads // 2
+
+    def swap(which):
+        mine = pl.ds((core if which else 1 - core) * own_heads, own_heads)
+        return pltpu.make_async_remote_copy(
+            src_ref=tx0.at[mine],
+            dst_ref=rx0.at[mine],
+            send_sem=pair_sem.at[which],
+            recv_sem=pair_sem.at[2 + which],
+            device_id={"seq": partner, "head": me_h},
+            device_id_type=MESH,
+        )
+
+    swap(0).start()
+    swap(1).start()
+    swap(0).wait_recv()
+
     slices = n_chip // heads
     slab = SUB // slices
     for i in range(own_heads):
@@ -477,7 +500,7 @@
         state0 = initt_ref[pl.ds(pl.multiple_of(my_part * slab, slab), slab)]
 
         def chain(i, state):
-            tx2[i] = state
+            tx2[i] = state.astype(BF16)
             for other_core in (0, 1):
 
                 @pl.when(2 * i + other_core != me_s)
@@ -505,20 +528,21 @@
 
     @pl.when(handling)
     def _():
-        b_bytes = partial_ref.at[pl.ds(0, (n_chip - 1) * slab // 2), pl.ds(0, 2 * SUB)]
+        b_bytes = reach_ref.at[pl.ds(0, (n_chip - 1) * slab), pl.ds(0, SUB)]
         pltpu.make_async_copy(b_bytes, b_bytes, b_recv.at[0]).wait()
 
     @pl.when(jnp.logical_not(handling))
     def _():
-        b_bytes = partial_ref.at[pl.ds(0, n_chip * slab // 2), pl.ds(0, 2 * SUB)]
+        b_bytes = inc_ref
         pltpu.make_async_copy(b_bytes, b_bytes, b_recv.at[0]).wait()
 
+    swap(1).wait_recv()
     for h in range(heads):
-        came = inc_ref[h]
+        came = inc_ref[h].astype(F32)
         first = rx0[h]
         stepped = (
             joined3(first[SUB : SUB + 16]) * came
-            - mm(came.astype(BF16), first[:SUB])
+            - mm(inc_ref[h], first[:SUB])
             + first[SUB + 16 :].astype(F32)
         )
         flag = (jnp.zeros((1, 1), jnp.int32) + core) == 0
@@ -532,6 +556,8 @@
         )
         closing_ref[0, h] = closing.T
 
+    swap(0).wait_send()
+    swap(1).wait_send()
     ring_bytes = gbuf.at[pl.ds(0, tokens), pl.ds(0, (n_head - 1) * width)]
     pltpu.make_async_copy(ring_bytes, ring_bytes, sent_sem.at[0]).wait()
     pltpu.make_async_copy(halo_bytes, halo_bytes, sent_sem.at[1]).wait()
@@ -542,7 +568,7 @@
     def _():
         a_bytes = rx1.at[pl.ds(0, messages - 1)]
         pltpu.make_async_copy(a_bytes, a_bytes, sent_sem.at[2]).wait()
-        b_bytes = partial_ref.at[pl.ds(0, (n_seq - 1) * slab // 2), pl.ds(0, 2 * SUB)]
+        b_bytes = gbuf.at[pl.ds(0, (n_seq - 1) * slab // 2), pl.ds(0, 2 * SUB)]
         pltpu.make_async_copy(b_bytes, b_bytes, sent_sem.at[3]).wait()
 
     @pl.when(jnp.logical_not(handling))
@@ -584,7 +610,7 @@
                 pltpu.VMEM(cv.shape, BF16),
                 pltpu.VMEM((tokens + HALO, columns), F32),
                 pltpu.VMEM((4, columns), F32),
-                pltpu.VMEM((len(LEVELS), SUB, SUB), BF16),
+                pltpu.VMEM((len(LEVELS) + 2, SUB, SUB), BF16),
                 pltpu.VMEM((heads, SUB, 2 * SUB), F32),
                 pltpu.VMEM((heads, 8, SUB), F32),
                 pltpu.VMEM((blocks * heads, SUB, SUB), F32),
@@ -600,14 +626,14 @@
                 pltpu.VMEM((heads, 2 * SUB + 16, SUB), BF16),
                 pltpu.VMEM((heads // 2, slices, SUB + 16 + slab, SUB), BF16),
                 pltpu.VMEM((n_chip, SUB + 16 + slab, SUB), BF16),
-                pltpu.VMEM((n_chip, slab, SUB), F32),
-                pltpu.VMEM((heads, SUB, SUB), F32),
+                pltpu.VMEM((n_chip, slab, SUB), BF16),
+                pltpu.VMEM((heads, SUB, SUB), BF16),
                 pltpu.VMEM((SUB, SUB), F32),
                 dma((10,)),
                 dma((4,)),
                 dma((2, 2 * blocks, n_head // 2)),
-                dma((1,)),
-                dma((2,)),
+                dma((2, n_head // 2 + 1)),
+                dma((4,)),
                 dma((n_chip,)),
                 dma((1,)),
             ],

time: 61 us -> 58.5 us (0.959)
  Pallas kernels: 56.6 us -> 54.1 us
    pallas_call x1, Pallas kernels: 56.6 us -> 54.1 us  [body(): pl.pallas_call(functools.partial(kernel, n_seq, n_head), out_shape=(jax.S...]
where the time goes in v3:
time: 58.5 us; the launch traced here: 58.3 us
  Pallas kernels  54.1 us (92%)
  local copies, waits for them, and re-layouts  3.54 us (6%)
  between operations  0.64 us (1%)
    pallas_call x1, Pallas kernels, body(): pl.pallas_call(functools.partial(kernel, n_seq, n_head), out_shape=(jax.S...  54.1 us
    unnamed x2, local copies, waits for them, and re-layouts  3.54 us

profile of v3, /device:TPU:7, one launch (start us, length us, event | category | flops | bytes accessed | tf_op | source)
XLA Modules:
  0.0 58.3 jit_solution(1919656275435936174)
XLA Ops:
  0.6 54.1 %shard_map.113 = (bf16[512,512]{1,0:T(8,128)(2,1)}, f32[1,4,128,128]{3,2,1,0:T(8,128)}) custom-call(bf16[512,256]{1,0:T(8,128)(2,1)} %hidden_ref.1, bf16[2048,256]{1,0:T(8,128)(2,1)} %wq_ref.1, bf16[2048,256]{1,0:T(8,128)(2,1)} %wk_ref.1, bf16[2048,512]{1,0:T(8,128)(2,1)} %wv_ref.1, bf16[4,256]{1,0:T(4,128)(2,1)} %cq_hbm.1, bf16[4,256]{1,0:T(4,128)(2,1)} %ck_hbm.1, ...), custom_call_target="tpu_custom_call" | custom-call | tf_op jit(solution)/shard_map/pallas_call | solution.py:594
  54.8 1.9 %copy.14 = bf16[512,512]{1,0:T(8,128)(2,1)} copy(bf16[512,512]{1,0:T(8,128)(2,1)} %get-tuple-element.4) | data formatting | bytes 1048576
  56.6 1.7 %copy.15 = f32[1,4,128,128]{3,2,1,0:T(8,128)} copy(f32[1,4,128,128]{3,2,1,0:T(8,128)} %get-tuple-element.5) | data formatting | bytes 524288

commit v4 on v3

--- a/solution.py
+++ b/solution.py
@@ -14,12 +14,12 @@
 HALO = 16
 LEVELS = (2, 4, 8, 16, 32, 64)
 FIRST = (
-    (0, 0, 0), (1, 1, 0), (1, 0, 0), (2, 0, 0), (0, 1, 0), (0, 0, 1), (1, 1, 1),
-    (1, 0, 1), (3, 0, 0), (0, 1, 1), (0, 0, 2), (3, 1, 0), (1, 0, 2), (2, 0, 1),
-    (3, 0, 1), (0, 1, 2), (2, 1, 0), (0, 0, 3), (1, 1, 2), (1, 0, 3), (2, 0, 2),
-    (2, 1, 1), (3, 0, 2), (3, 1, 1),
+    (0, 0, 0), (0, 1, 0), (1, 0, 0), (2, 1, 0), (3, 0, 0), (2, 0, 0), (0, 0, 1),
+    (1, 1, 0), (1, 0, 1), (2, 1, 1), (3, 1, 0), (0, 1, 1), (0, 0, 2), (1, 1, 1),
+    (1, 0, 2), (3, 0, 1), (2, 0, 1), (0, 1, 2), (0, 0, 3), (3, 1, 1), (1, 1, 2),
+    (1, 0, 3), (2, 0, 2), (3, 0, 2), (2, 1, 2),
 )
-BESIDE = ((4, 2, 0, 3), (5, 2, 1, 2), (6, 3, 0, 3), (7, 3, 1, 2))
+BESIDE = ((2, 3, 1, 2), (5, 2, 0, 3), (5, 3, 0, 3),)
 HALO_AFTER = (5, 10, 15, 20)
 NT = (((1,), (1,)), ((), ()))
 
@@ -273,6 +273,32 @@
         rows = gbuf[pl.ds(start, size), :]
         x_ref[pl.ds(place, size), columns] = mm(rows, w_ref[:, columns]).astype(BF16).astype(F32)
 
+    def owner_columns(steps):
+        return [
+            pl.ds(pl.multiple_of(lax.rem(me_h + step, n_head) * width, width), width)
+            for step in steps
+        ]
+
+    def gathered(start, size, columns):
+        return jnp.concatenate([gbuf[pl.ds(start, size), c] for c in columns], axis=1)
+
+    def weights(owners, columns):
+        return jnp.concatenate([w_ref[c, columns] for c in owners], axis=0)
+
+    NEAR, FAR = (0, 1, n_head - 1), tuple(range(2, n_head - 1))
+
+    def project_near(n):
+        owners = owner_columns(NEAR)
+        rows = gathered(n * SUB, SUB, owners)
+        x_ref[pl.ds(n * SUB + HALO, SUB), :] = mm(rows, weights(owners, slice(None)))
+
+    def project_far(start, place, columns):
+        owners = owner_columns(FAR)
+        total = x_ref[pl.ds(place, SUB), columns] + mm(
+            gathered(start, SUB, owners), weights(owners, columns)
+        )
+        x_ref[pl.ds(place, SUB), columns] = total.astype(BF16).astype(F32)
+
     def start_conv():
         tap_ref[:, :qcols] = cq_ref[...].astype(F32)
         tap_ref[:, qcols : 2 * qcols] = ck_ref[...].astype(F32)
@@ -293,6 +319,9 @@
         if index in (5, 9, 12, 15):
             prepare((5, 9, 12, 15).index(index))
         event(*entry)
+        for n in range(blocks):
+            if index == max(FIRST.index((n, 0, 1)), FIRST.index((n, 1, 1))):
+                project_near(n)
         if index in HALO_AFTER:
             halo_event(HALO_AFTER.index(index))
     def conv(base, columns):
@@ -317,7 +346,7 @@
         for part in range(2):
             service(pair, stage + part)
             columns = slice(part * 2 * qcols, part * 2 * qcols + 2 * qcols)
-            project(base, SUB, base + HALO, columns)
+            project_far(base, base + HALO, columns)
 
     def systems(n):
         base = n * SUB
@@ -428,6 +457,34 @@
 
     slices = n_chip // heads
     slab = SUB // slices
+    def job(q):
+        part = lax.div(q, heads)
+        head = lax.rem(part + q, heads)
+        return part, head
+
+    def to_handler(q):
+        part, head = job(q)
+        return pltpu.make_async_remote_copy(
+            src_ref=tx1.at[lax.rem(head, own_heads), part],
+            dst_ref=rx1.at[chip],
+            send_sem=sent_sem.at[2],
+            recv_sem=a_recv.at[chip],
+            device_id={"seq": 2 * q + core, "head": me_h},
+            device_id_type=MESH,
+        )
+
+    def for_me(q):
+        return lax.div(job(q)[1], own_heads) == core
+
+    def send_a(i, k, carry):
+        q = chip ^ k
+
+        @pl.when((q != chip) & (job(q)[1] == core * own_heads + i))
+        def _():
+            to_handler(q).start()
+
+        return carry
+
     for i in range(own_heads):
         h = core * own_heads + i
         mine, other = tx0[h], rx0[h]
@@ -446,36 +503,8 @@
             tx1[i, part, :SUB] = c_new
             tx1[i, part, SUB : SUB + 16] = g_new
             tx1[i, part, SUB + 16 :] = s_new[slab * part : slab * part + slab]
-
-    def job(q):
-        part = lax.div(q, heads)
-        head = lax.rem(part + q, heads)
-        return part, head
-
-    def to_handler(q):
-        part, head = job(q)
-        return pltpu.make_async_remote_copy(
-            src_ref=tx1.at[lax.rem(head, own_heads), part],
-            dst_ref=rx1.at[chip],
-            send_sem=sent_sem.at[2],
-            recv_sem=a_recv.at[chip],
-            device_id={"seq": 2 * q + core, "head": me_h},
-            device_id_type=MESH,
-        )
-
-    def for_me(q):
-        return lax.div(job(q)[1], own_heads) == core
-
-    def send_a(k, carry):
-        q = chip ^ k
-
-        @pl.when((q != chip) & for_me(q))
-        def _():
-            to_handler(q).start()
-
-        return carry
-
-    lax.fori_loop(0, n_chip, send_a, 0)
+        lax.fori_loop(0, n_chip, functools.partial(send_a, i), 0)
+
     my_part, my_head = job(chip)
     handling = for_me(chip)
 

time: 58.5 us -> 57.5 us (0.983)
  Pallas kernels: 54.1 us -> 53.2 us
    pallas_call x1, Pallas kernels: 54.1 us -> 53.2 us  [body(): pl.pallas_call(functools.partial(kernel, n_seq, n_head), out_shape=(jax.S...]
where the time goes in v4:
time: 57.5 us; the launch traced here: 57.4 us
  Pallas kernels  53.2 us (93%)
  local copies, waits for them, and re-layouts  3.54 us (6%)
  between operations  0.64 us (1%)
    pallas_call x1, Pallas kernels, body(): pl.pallas_call(functools.partial(kernel, n_seq, n_head), out_shape=(jax.S...  53.2 us
    unnamed x2, local copies, waits for them, and re-layouts  3.54 us

profile of v4, /device:TPU:7, one launch (start us, length us, event | category | flops | bytes accessed | tf_op | source)
XLA Modules:
  0.0 57.4 jit_solution(6009347786252018169)
XLA Ops:
  0.6 53.2 %shard_map.113 = (bf16[512,512]{1,0:T(8,128)(2,1)}, f32[1,4,128,128]{3,2,1,0:T(8,128)}) custom-call(bf16[512,256]{1,0:T(8,128)(2,1)} %hidden_ref.1, bf16[2048,256]{1,0:T(8,128)(2,1)} %wq_ref.1, bf16[2048,256]{1,0:T(8,128)(2,1)} %wk_ref.1, bf16[2048,512]{1,0:T(8,128)(2,1)} %wv_ref.1, bf16[4,256]{1,0:T(4,128)(2,1)} %cq_hbm.1, bf16[4,256]{1,0:T(4,128)(2,1)} %ck_hbm.1, ...), custom_call_target="tpu_custom_call" | custom-call | tf_op jit(solution)/shard_map/pallas_call | solution.py:623
  53.8 1.9 %copy.14 = bf16[512,512]{1,0:T(8,128)(2,1)} copy(bf16[512,512]{1,0:T(8,128)(2,1)} %get-tuple-element.4) | data formatting | bytes 1048576
  55.7 1.7 %copy.15 = f32[1,4,128,128]{3,2,1,0:T(8,128)} copy(f32[1,4,128,128]{3,2,1,0:T(8,128)} %get-tuple-element.5) | data formatting | bytes 524288

commit v5 on v4

--- a/solution.py
+++ b/solution.py
@@ -285,15 +285,18 @@
     def weights(owners, columns):
         return jnp.concatenate([w_ref[c, columns] for c in owners], axis=0)
 
-    NEAR, FAR = (0, 1, n_head - 1), tuple(range(2, n_head - 1))
+    def reach_of(n):
+        return 2 if n < 2 else 1
+
 
     def project_near(n):
-        owners = owner_columns(NEAR)
+        reach = reach_of(n)
+        owners = owner_columns(range(-reach + n_head, reach + n_head + 1))
         rows = gathered(n * SUB, SUB, owners)
         x_ref[pl.ds(n * SUB + HALO, SUB), :] = mm(rows, weights(owners, slice(None)))
 
-    def project_far(start, place, columns):
-        owners = owner_columns(FAR)
+    def project_far(n, start, place, columns):
+        owners = owner_columns(range(reach_of(n) + 1, n_head - reach_of(n)))
         total = x_ref[pl.ds(place, SUB), columns] + mm(
             gathered(start, SUB, owners), weights(owners, columns)
         )
@@ -320,7 +323,8 @@
             prepare((5, 9, 12, 15).index(index))
         event(*entry)
         for n in range(blocks):
-            if index == max(FIRST.index((n, 0, 1)), FIRST.index((n, 1, 1))):
+            hops = reach_of(n)
+            if index == max(FIRST.index((n, 0, hops)), FIRST.index((n, 1, hops))):
                 project_near(n)
         if index in HALO_AFTER:
             halo_event(HALO_AFTER.index(index))
@@ -346,7 +350,7 @@
         for part in range(2):
             service(pair, stage + part)
             columns = slice(part * 2 * qcols, part * 2 * qcols + 2 * qcols)
-            project_far(base, base + HALO, columns)
+            project_far(n, base, base + HALO, columns)
 
     def systems(n):
         base = n * SUB

time: 57.5 us -> 57.6 us (level)
  no operation moved by 1% of the time
where the time goes in v5:
time: 57.6 us; the launch traced here: 57.4 us
  Pallas kernels  53.2 us (92%)
  local copies, waits for them, and re-layouts  3.54 us (6%)
  between operations  0.64 us (1%)
    pallas_call x1, Pallas kernels, body(): pl.pallas_call(functools.partial(kernel, n_seq, n_head), out_shape=(jax.S...  53.2 us
    unnamed x2, local copies, waits for them, and re-layouts  3.54 us

profile of v5, /device:TPU:7, one launch (start us, length us, event | category | flops | bytes accessed | tf_op | source)
XLA Modules:
  0.0 57.4 jit_solution(1754220026526476524)
XLA Ops:
  0.6 53.2 %shard_map.113 = (bf16[512,512]{1,0:T(8,128)(2,1)}, f32[1,4,128,128]{3,2,1,0:T(8,128)}) custom-call(bf16[512,256]{1,0:T(8,128)(2,1)} %hidden_ref.1, bf16[2048,256]{1,0:T(8,128)(2,1)} %wq_ref.1, bf16[2048,256]{1,0:T(8,128)(2,1)} %wk_ref.1, bf16[2048,512]{1,0:T(8,128)(2,1)} %wv_ref.1, bf16[4,256]{1,0:T(4,128)(2,1)} %cq_hbm.1, bf16[4,256]{1,0:T(4,128)(2,1)} %ck_hbm.1, ...), custom_call_target="tpu_custom_call" | custom-call | tf_op jit(solution)/shard_map/pallas_call | solution.py:627
  53.9 1.9 %copy.14 = bf16[512,512]{1,0:T(8,128)(2,1)} copy(bf16[512,512]{1,0:T(8,128)(2,1)} %get-tuple-element.4) | data formatting | bytes 1048576
  55.8 1.7 %copy.15 = f32[1,4,128,128]{3,2,1,0:T(8,128)} copy(f32[1,4,128,128]{3,2,1,0:T(8,128)} %get-tuple-element.5) | data formatting | bytes 524288
